TPU v7x, 256 devices: a whole 4x4x8 slice. The times are simulated.
256 devices in a mesh: lat: 4 (over x_lo, core), lon: 64 (over y, z, x_hi).
Axes of the slice: x: 4 (x_hi: 2, x_lo: 2; x = x_hi * 2 + x_lo), y: 4, z: 8, core: 2. Of those that a mesh axis runs over, the one named last changes fastest.
Arguments:
- prognostic: float32 [5, 8, 2880, 1440], P(None, None, 'lon', 'lat'), may hold values from -6 to 6
- filter_rows: int32 [128], replicated, may hold values from 0 to 1439, as said below
- cutoff: int32 [128], replicated, may hold values from 360 to 1439
Outputs:
- advanced: float32 [5, 8, 2880, 1440], P(None, None, 'lon', 'lat')
Inputs may be any that keep to these rules, and one draw needn't show every extreme that they name: `filter_rows`: the first 64 entries are distinct rows of the southern band (0 to 359) in rising order, always including row 0; the last 64 are distinct rows of the northern band (1080 to 1439) in rising order, always including row 1439.
All inputs are finite; a program needn't handle non-finite values.
Results may differ from a plain program's by a relative error of at most 0.0001.
Values sent between devices are 32-bit elements; how exact they have to be, the bound alone decides.
No kernel may reach another device: no remote copies, remote signals or barrier semaphores. Data moves between devices by JAX's collectives and lax.ppermute only.
A program may use at most 192 MiB of HBM per device.

v0:
```python
import jax
import jax.numpy as jnp
from jax import lax
from jax.sharding import PartitionSpec as P

SUBSTEPS = 2


meridional_courant = 0.5
vertical_courant = 0.5
buoyancy_rate = 0.3
polar_courant = 0.5
coriolis_rate = 0.2


def padded_2(cells, sides, width):
    for axis, dim in sides:
        count = lax.axis_size(axis)
        head = lax.slice_in_dim(cells, 0, width, axis=dim)
        tail = lax.slice_in_dim(cells, cells.shape[dim] - width, cells.shape[dim], axis=dim)
        cells = jnp.concatenate(
            [
                lax.ppermute(tail, axis, [(i, (i + 1) % count) for i in range(count)]),
                cells,
                lax.ppermute(head, axis, [((i + 1) % count, i) for i in range(count)]),
            ],
            axis=dim,
        )
    return cells


def shifted(value, axis, steps):
    count = lax.axis_size(axis)
    pairs = [(source, (source + steps) % count) for source in range(count)]
    return lax.ppermute(value, axis, pairs)


def row_angles(first, row_total, length):
    position = (first + jnp.arange(length)).astype(jnp.float32)
    return (position + 0.5) * (jnp.pi / row_total)


def vertical_difference(field):
    padded = jnp.pad(field, ((1, 1), (0, 0), (0, 0)))
    return (padded[2:] - padded[:-2]) * 0.5


def fourier_table(length):
    position = jnp.arange(length, dtype=jnp.int32)
    wavenumber = position[: length // 2]
    phase = position[:, None] * wavenumber[None, :] % length
    phase_angle = phase.astype(jnp.float32) * (2.0 * jnp.pi / length)
    return jnp.concatenate([jnp.cos(phase_angle), jnp.sin(phase_angle)], axis=1)


def pole_extend(field, sign_flip, lat_id, lat_count):
    extended = padded_2(field, (("lat", 3), ("lon", 2)), 1)
    edge_rows = jnp.concatenate([field[..., :1], field[..., -1:]], axis=3)
    across = shifted(edge_rows, "lon", lax.axis_size("lon") // 2) * sign_flip
    southern = jnp.where(lat_id == 0, across[..., 0], extended[:, :, 1:-1, 0])
    northern = jnp.where(lat_id == lat_count - 1, across[..., 1], extended[:, :, 1:-1, -1])
    extended = extended.at[:, :, 1:-1, 0].set(southern)
    return extended.at[:, :, 1:-1, -1].set(northern)


def acoustic_update(state, cosine, sine_lat, polar_cos, lat_id, lat_count):
    zonal_wind = state[0]
    north_wind = state[1]
    vertical = state[2]
    pressure = state[3]
    potential = state[4]
    zonal_courant = polar_courant * polar_cos / cosine[1:-1]
    coriolis = coriolis_rate * sine_lat[1:-1]
    pressure_pad = pole_extend(pressure[None], 1.0, lat_id, lat_count)[0]
    zonal_gradient = (pressure_pad[:, 2:, 1:-1] - pressure_pad[:, :-2, 1:-1]) * 0.5
    north_gradient = (pressure_pad[:, 1:-1, 2:] - pressure_pad[:, 1:-1, :-2]) * 0.5
    zonal_next = zonal_wind - zonal_courant * zonal_gradient + coriolis * north_wind
    north_next = north_wind - meridional_courant * north_gradient - coriolis * zonal_wind
    vertical_next = (
        vertical - vertical_courant * vertical_difference(pressure) + buoyancy_rate * potential
    )
    winds = pole_extend(jnp.stack([zonal_next, north_next]), -1.0, lat_id, lat_count)
    zonal_change = (winds[0, :, 2:, 1:-1] - winds[0, :, :-2, 1:-1]) * 0.5
    north_flux = winds[1] * cosine
    north_change = (north_flux[:, 1:-1, 2:] - north_flux[:, 1:-1, :-2]) * 0.5 / cosine[1:-1]
    divergence = (
        zonal_courant * zonal_change
        + meridional_courant * north_change
        + vertical_courant * vertical_difference(vertical_next)
    )
    pressure_next = pressure - divergence
    potential_next = potential - buoyancy_rate * vertical_next
    return jnp.stack([zonal_next, north_next, vertical_next, pressure_next, potential_next])


def filter_items(item_data, limit_items, fourier):
    row_data = lax.all_to_all(item_data, "lon", split_axis=0, concat_axis=1, tiled=True)
    limits = lax.all_to_all(limit_items, "lon", split_axis=0, concat_axis=1, tiled=True)
    full_rows = row_data[0]
    keep_limit = limits[0, :1, :]
    length = full_rows.shape[0]
    halfway = length // 2
    wavenumber = jnp.arange(length, dtype=jnp.int32) % halfway
    scale = jnp.where(wavenumber == 0, 1.0, 2.0) / length
    weight = jnp.where(wavenumber[:, None].astype(jnp.float32) <= keep_limit, scale[:, None], 0.0)
    spectrum = jnp.einsum(
        "nk,ni->ki",
        fourier,
        full_rows,
        precision=lax.Precision.HIGHEST,
        preferred_element_type=jnp.float32,
    )
    restored = jnp.einsum(
        "nk,ki->ni",
        fourier,
        spectrum * weight,
        precision=lax.Precision.HIGHEST,
        preferred_element_type=jnp.float32,
    )
    return lax.all_to_all(restored[None], "lon", split_axis=1, concat_axis=0, tiled=True)


def filter_state(state, filter_rows, cutoff, lat_id, lat_count, fourier):
    fields, levels, columns, rows_dev = state.shape
    flag_count = filter_rows.shape[0] // 2
    lon_count = lax.axis_size("lon")
    northern = lat_id == lat_count - 1
    polar_band = (lat_id == 0) | northern
    chosen = (
        jnp.where(northern, filter_rows[flag_count:], filter_rows[:flag_count]) - lat_id * rows_dev
    )
    chosen = jnp.clip(chosen, 0, rows_dev - 1)
    limits = jnp.where(northern, cutoff[flag_count:], cutoff[:flag_count]).astype(jnp.float32)
    picked = jnp.take(state, chosen, axis=3)
    item_data = picked.transpose(2, 0, 1, 3).reshape(columns, lon_count, -1).transpose(1, 0, 2)
    limit_items = jnp.broadcast_to(limits[None, None, :], (fields, levels, flag_count)).reshape(
        lon_count, 1, -1
    )
    result = filter_items(item_data, limit_items, fourier)
    result = (
        result.transpose(1, 0, 2).reshape(columns, fields, levels, flag_count).transpose(1, 2, 0, 3)
    )
    replaced = jnp.where(polar_band, result, picked)
    return state.at[:, :, :, chosen].set(replaced)


def per_device(prognostic, filter_rows, cutoff):
    fields, levels, columns, rows_dev = prognostic.shape
    lat_count = lax.axis_size("lat")
    lon_count = lax.axis_size("lon")
    lat_id = lax.axis_index("lat")
    row_total = rows_dev * lat_count
    phase_angle = row_angles(lat_id * rows_dev - 1, row_total, rows_dev + 2)
    cosine = jnp.abs(jnp.sin(phase_angle))
    sine_lat = -jnp.cos(phase_angle)
    polar_cos = jnp.abs(jnp.sin(row_angles(0, row_total, 1)))[0]
    fourier = fourier_table(columns * lon_count)
    state = prognostic
    for substep_index in range(SUBSTEPS):
        state = acoustic_update(state, cosine, sine_lat, polar_cos, lat_id, lat_count)
        state = filter_state(state, filter_rows, cutoff, lat_id, lat_count, fourier)
    return state


def solution(mesh):
    in_specs = (P(None, None, "lon", "lat"), P(), P())
    out_specs = P(None, None, "lon", "lat")
    return jax.shard_map(
        per_device, mesh=mesh, in_specs=in_specs, out_specs=out_specs, check_vma=False
    )
```

profile of v0, /device:TPU:8, one launch (start us, length us, event | category | flops | bytes accessed | tf_op | source)
XLA Modules:
  0.0 555.8 jit_solution(12315603337750878246)
XLA Ops:
  1.5 14.8 %all-to-all-start.1 = ((f32[64,1,40]{2,1,0:T(1,128)}), f32[64,1,40]{2,1,0:T(1,128)}, u32[]{:S(2)}, u32[]{:S(2)}) async-start(f32[64,1,40]{2,1,0:T(1,128)} %bitcast.18), calls=%async_computation.1 | async-start | bytes 65536 | tf_op jit(solution)/shard_map/all_to_all | solution.py:98
  20.7 2.9 fusion.92
  26.2 3.1 copy.186
  35.7 3.0 collective-permute-start.2
  38.7 3.6 collective-permute-start.3
  46.6 3.8 constant_dynamic-update-slice_fusion.1
  64.1 4.9 collective-permute-start.8
  77.2 3.0 fusion.24
  81.5 3.9 gather_fusion
  91.1 3.3 reshape.485
  94.4 12.3 %all-to-all-start = ((f32[64,1,1800]{2,1,0:T(1,128)}), f32[64,1,1800]{2,1,0:T(1,128)S(1)}, u32[]{:S(2)}, u32[]{:S(2)}) async-start(f32[64,1,1800]{2,1,0:T(1,128)} %reshape.485), calls=%async_computation | async-start | bytes 983040 | tf_op jit(solution)/shard_map/all_to_all | solution.py:97
  106.6 75.4 %fusion.5 = (f32[2880,1440]{1,0:T(8,128)}, f32[2880,1440]{1,0:T(8,128)}) fusion(s32[1440]{0:T(1024)S(1)} %iota_add_fusion), kind=kLoop, calls=%fused_computation.12 | loop fusion | flops 37324800 | bytes 33183360 | tf_op jit(solution)/shard_map/cos | solution.py:53
  188.9 28.1 %fusion.11 = f32[2880,40]{0,1:T(8,128)S(1)} fusion(f32[2880,40]{0,1:T(8,128)S(1)} %squeeze.82, f32[2880,1440]{1,0:T(8,128)} %get-tuple-element.145, f32[2880,1440]{1,0:T(8,128)} %get-tuple-element.144, f32[2880]{0:T(1024)S(1)} %select_multiply_fusion, f32[2880]{0:T(1024)S(1)} %fusion.68, f32[40]{0:T(128)S(1)} %slice_bitcast_fusion.6), kind=kOutput, calls=%fused_computation.36 | convolution fusion | flops 3989952000 | bytes 34122400 | tf_op jit(solution)/shard_map/nk,ni->ki/dot_general | solution.py:106
  217.0 32.0 %fusion.9 = f32[2880,40]{1,0:T(8,128)} fusion(f32[2880,40]{0,1:T(8,128)S(1)} %fusion.11, f32[2880,1440]{1,0:T(8,128)} %get-tuple-element.145, f32[2880,1440]{1,0:T(8,128)} %get-tuple-element.144), kind=kOutput, calls=%fused_computation.16 | convolution fusion | flops 3989606400 | bytes 34099200 | tf_op jit(solution)/shard_map/nk,ki->ni/dot_general | solution.py:113
  249.0 13.9 %reduce.17 = f32[2880,40]{1,0:T(8,128)S(1)} reduce(f32[2880,1,40]{2,1,0:T(1,128)} %bitcast.190, f32[]{:T(128)} %broadcast.293), dimensions={1}, to_apply=%bitcast.148.reduce_sub_computation | reduce | bytes 921604
  265.1 12.7 %all-to-all-start.2 = ((f32[64,1,1800]{2,1,0:T(1,128)}), f32[64,1,1800]{2,1,0:T(1,128)S(1)}, u32[]{:S(2)}, u32[]{:S(2)}) async-start(f32[64,1,1800]{2,1,0:T(1,128)} %reshape.487), calls=%async_computation.2 | async-start | bytes 983040 | tf_op jit(solution)/shard_map/all_to_all | solution.py:120
  277.9 15.7 %all-to-all-done.2 = f32[64,1,1800]{2,1,0:T(1,128)S(1)} async-done(((f32[64,1,1800]{2,1,0:T(1,128)}), f32[64,1,1800]{2,1,0:T(1,128)S(1)}, u32[]{:S(2)}, u32[]{:S(2)}) %all-to-all-start.2) | async-done | bytes 460832 | tf_op jit(solution)/shard_map/all_to_all | solution.py:120
  309.2 9.2 %scatter_fusion = f32[5,8,45,360]{2,1,3,0:T(8,128)} fusion(f32[5,8,45,360]{2,1,3,0:T(8,128)} %bitcast_dynamic-update-slice_fusion.2, s32[64]{0:T(128)S(1)} %copy-done.14, f32[64,5,8,45]{3,2,1,0:T(8,128)} %fusion.64), kind=kCustom, calls=%fused_computation.2 | custom fusion | bytes 1382656 | tf_op jit(solution)/shard_map/scatter | solution.py:144
  326.9 5.4 collective-permute-start.13
  335.1 3.6 constant_dynamic-update-slice_fusion.3
  338.8 3.7 constant_dynamic-update-slice_fusion.2
  345.9 3.9 bitcast_dynamic-update-slice_fusion.1
  355.5 5.6 %collective-permute-start.18 = (f32[2,8,1,362]{3,1,2,0:T(8,128)S(1)}, f32[2,8,1,362]{3,1,2,0:T(8,128)S(1)}, u32[]{:S(2)}, u32[]{:S(2)}) collective-permute-start(f32[2,8,1,362]{3,1,2,0:T(8,128)S(1)} %get-tuple-element.131), channel_id=1, source_target_pairs={{1,0},{2,1},{3,2},{4,3},{5,4},{6,5},{7,6},{8,7},{9,8},{10,9},{11,1... | collective-permute-start | bytes 69512 | tf_op jit(solution)/shard_map/ppermute | solution.py:25
  368.6 4.6 fusion.34
  376.0 3.9 gather_fusion.1
  388.1 29.9 %all_to_all.29 = f32[64,1,1800]{2,1,0:T(1,128)S(1)} all-to-all(f32[64,1,1800]{2,1,0:T(1,128)S(1)} %reshape.489), channel_id=1, replica_groups=mesh['lat'=4,'lon'=64] {'lon'}, dimensions={0} | all-to-all | bytes 921600 | tf_op jit(solution)/shard_map/all_to_all | solution.py:97
  423.6 28.1 %fusion.12 = f32[2880,40]{0,1:T(8,128)S(1)} fusion(f32[2880,40]{0,1:T(8,128)S(1)} %squeeze.91, f32[2880,1440]{1,0:T(8,128)} %get-tuple-element.145, f32[2880,1440]{1,0:T(8,128)} %get-tuple-element.144, f32[2880]{0:T(1024)S(1)} %select_multiply_fusion, f32[2880]{0:T(1024)S(1)} %fusion.68, f32[40]{0:T(128)S(1)} %slice_bitcast_fusion.6), kind=kOutput, calls=%fused_computation.37 | convolution fusion | flops 3989952000 | bytes 34122400 | tf_op jit(solution)/shard_map/nk,ni->ki/dot_general | solution.py:106
  451.7 32.1 %fusion.7 = f32[2880,40]{1,0:T(8,128)} fusion(f32[2880,40]{0,1:T(8,128)S(1)} %fusion.12, f32[2880,1440]{1,0:T(8,128)} %get-tuple-element.145, f32[2880,1440]{1,0:T(8,128)} %get-tuple-element.144), kind=kOutput, calls=%fused_computation.14 | convolution fusion | flops 3989606400 | bytes 34099200 | tf_op jit(solution)/shard_map/nk,ki->ni/dot_general | solution.py:113
  483.8 13.9 %reduce.20 = f32[2880,40]{1,0:T(8,128)S(1)} reduce(f32[2880,1,40]{2,1,0:T(1,128)} %bitcast.189, f32[]{:T(128)} %broadcast.293), dimensions={1}, to_apply=%bitcast.152.reduce_sub_computation | reduce | bytes 921604
  499.1 24.2 %all_to_all.60 = f32[64,1,1800]{2,1,0:T(1,128)S(1)} all-to-all(f32[64,1,1800]{2,1,0:T(1,128)S(1)} %reshape.491), channel_id=1, replica_groups=mesh['lat'=4,'lon'=64] {'lon'}, dimensions={0} | all-to-all | bytes 921600 | tf_op jit(solution)/shard_map/all_to_all | solution.py:120
  538.9 9.2 %scatter_fusion.1 = f32[5,8,45,360]{2,1,3,0:T(8,128)} fusion(f32[5,8,45,360]{2,1,3,0:T(8,128)} %bitcast_dynamic-update-slice_fusion, s32[64]{0:T(128)S(1)} %copy-done.14, f32[64,5,8,45]{3,2,1,0:T(8,128)} %fusion.63), kind=kCustom, calls=%fused_computation.3 | custom fusion | bytes 1382656 | tf_op jit(solution)/shard_map/scatter | solution.py:144
  548.1 7.2 %copy.180 = f32[5,8,45,360]{3,1,2,0:T(8,128)} copy(f32[5,8,45,360]{2,1,3,0:T(8,128)} %scatter_fusion.1) | data formatting | bytes 5184000 | tf_op jit(solution)/shard_map/scatter | solution.py:144
  (178 shorter events, 133.8 us)
Async XLA Ops:
  1.5 92.9 %all-to-all-start.1 = ((f32[64,1,40]{2,1,0:T(1,128)}), f32[64,1,40]{2,1,0:T(1,128)}, u32[]{:S(2)}, u32[]{:S(2)}) async-start(f32[64,1,40]{2,1,0:T(1,128)} %bitcast.18), calls=%async_computation.1 | async-start | bytes 65536 | tf_op jit(solution)/shard_map/all_to_all | solution.py:98
  17.5 17.9 %collective-permute-start.1 = (f32[1,8,45,1]{2,1,3,0:T(8,128)S(1)}, f32[1,8,45,1]{2,1,3,0:T(8,128)S(1)}, u32[]{:S(2)}, u32[]{:S(2)}) collective-permute-start(f32[1,8,45,1]{2,1,3,0:T(8,128)S(1)} %copy.184), channel_id=1, source_target_pairs={{64,0},{128,64},{192,128},{0,192},{65,1},{129,65},{193,129},{1,193... | collective-permute-start | bytes 4328 | tf_op jit(solution)/shard_map/ppermute | solution.py:25
  17.8 17.5 %collective-permute-start = (f32[1,8,45,1]{2,1,3,0:T(8,128)S(1)}, f32[1,8,45,1]{2,1,3,0:T(8,128)S(1)}, u32[]{:S(2)}, u32[]{:S(2)}) collective-permute-start(f32[1,8,45,1]{2,1,3,0:T(8,128)S(1)} %copy.182), channel_id=1, source_target_pairs={{0,64},{64,128},{128,192},{192,0},{1,65},{65,129},{129,193},{193,1... | collective-permute-start | bytes 4328 | tf_op jit(solution)/shard_map/ppermute | solution.py:23
  18.3 23.9 %collective-permute-start.4 = (f32[1,8,45,2]{2,1,3,0:T(8,128)S(1)}, f32[1,8,45,2]{2,1,3,0:T(8,128)S(1)}, u32[]{:S(2)}, u32[]{:S(2)}) collective-permute-start(f32[1,8,45,2]{2,1,3,0:T(8,128)S(1)} %pad_maximum_fusion.29), channel_id=1, source_target_pairs={{0,32},{1,33},{2,34},{3,35},{4,36},{5,37},{6,38},{7,39},{8,40},{9,... | collective-permute-start | bytes 8648 | tf_op jit(solution)/shard_map/ppermute | solution.py:35
  24.3 5.0 copy-start.13
  26.1 30.0 %copy-start = (f32[1,8,45,360]{2,1,3,0:T(8,128)}, f32[1,8,45,360]{2,1,3,0:T(8,128)S(1)}, u32[]{:S(2)}) copy-start(f32[1,8,45,360]{2,1,3,0:T(8,128)S(1)} %copy.183) | copy-start | bytes 1555204
  35.7 8.2 %collective-permute-start.2 = (f32[1,8,1,362]{3,1,2,0:T(8,128)S(1)}, f32[1,8,1,362]{3,1,2,0:T(8,128)S(1)}, u32[]{:S(2)}, u32[]{:S(2)}) collective-permute-start(f32[1,8,1,362]{3,1,2,0:T(8,128)S(1)} %get-tuple-element.136), channel_id=1, source_target_pairs={{0,1},{1,2},{2,3},{3,4},{4,5},{5,6},{6,7},{7,8},{8,9},{9,10},{10,1... | collective-permute-start | bytes 34760 | tf_op jit(solution)/shard_map/ppermute | solution.py:23
  38.7 5.2 collective-permute-start.3
  46.6 3.8 copy-start.4
  46.6 3.8 copy-start.5
  52.8 3.4 copy-start.6
  52.8 3.4 copy-start.10
  52.8 7.7 %collective-permute-start.5 = (f32[2,8,45,1]{2,1,3,0:T(8,128)S(1)}, f32[2,8,45,1]{2,1,3,0:T(8,128)S(1)}, u32[]{:S(2)}, u32[]{:S(2)}) collective-permute-start(f32[2,8,45,1]{2,1,3,0:T(8,128)S(1)} %get-tuple-element.121), channel_id=1, source_target_pairs={{0,64},{64,128},{128,192},{192,0},{1,65},{65,129},{129,193},{193,1... | collective-permute-start | bytes 8648 | tf_op jit(solution)/shard_map/ppermute | solution.py:23
  52.9 7.8 %collective-permute-start.6 = (f32[2,8,45,1]{2,1,3,0:T(8,128)S(1)}, f32[2,8,45,1]{2,1,3,0:T(8,128)S(1)}, u32[]{:S(2)}, u32[]{:S(2)}) collective-permute-start(f32[2,8,45,1]{2,1,3,0:T(8,128)S(1)} %get-tuple-element.122), channel_id=1, source_target_pairs={{64,0},{128,64},{192,128},{0,192},{65,1},{129,65},{193,129},{1,193... | collective-permute-start | bytes 8648 | tf_op jit(solution)/shard_map/ppermute | solution.py:25
  54.8 14.2 %collective-permute-start.9 = (f32[2,8,45,2]{2,1,3,0:T(8,128)S(1)}, f32[2,8,45,2]{2,1,3,0:T(8,128)S(1)}, u32[]{:S(2)}, u32[]{:S(2)}) collective-permute-start(f32[2,8,45,2]{2,1,3,0:T(8,128)S(1)} %pad_maximum_fusion.21), channel_id=1, source_target_pairs={{0,32},{1,33},{2,34},{3,35},{4,36},{5,37},{6,38},{7,39},{8,40},{9,... | collective-permute-start | bytes 17288 | tf_op jit(solution)/shard_map/ppermute | solution.py:35
  60.4 10.3 %copy-start.9 = (f32[2,8,45,360]{3,1,2,0:T(8,128)S(1)}, f32[2,8,45,360]{3,1,2,0:T(8,128)}, u32[]{:S(2)}) copy-start(f32[2,8,45,360]{3,1,2,0:T(8,128)} %copy.154) | copy-start | bytes 3110404
  61.8 8.9 %collective-permute-start.7 = (f32[2,8,1,362]{3,1,2,0:T(8,128)S(1)}, f32[2,8,1,362]{3,1,2,0:T(8,128)S(1)}, u32[]{:S(2)}, u32[]{:S(2)}) collective-permute-start(f32[2,8,1,362]{3,1,2,0:T(8,128)S(1)} %get-tuple-element.132), channel_id=1, source_target_pairs={{0,1},{1,2},{2,3},{3,4},{4,5},{5,6},{6,7},{7,8},{8,9},{9,10},{10,1... | collective-permute-start | bytes 69512 | tf_op jit(solution)/shard_map/ppermute | solution.py:23
  64.1 6.6 %collective-permute-start.8 = (f32[2,8,1,362]{3,1,2,0:T(8,128)S(1)}, f32[2,8,1,362]{3,1,2,0:T(8,128)S(1)}, u32[]{:S(2)}, u32[]{:S(2)}) collective-permute-start(f32[2,8,1,362]{3,1,2,0:T(8,128)S(1)} %get-tuple-element.133), channel_id=1, source_target_pairs={{1,0},{2,1},{3,2},{4,3},{5,4},{6,5},{7,6},{8,7},{9,8},{10,9},{11,1... | collective-permute-start | bytes 69512 | tf_op jit(solution)/shard_map/ppermute | solution.py:25
  81.5 3.9 copy-start.12
  94.4 88.4 %all-to-all-start = ((f32[64,1,1800]{2,1,0:T(1,128)}), f32[64,1,1800]{2,1,0:T(1,128)S(1)}, u32[]{:S(2)}, u32[]{:S(2)}) async-start(f32[64,1,1800]{2,1,0:T(1,128)} %reshape.485), calls=%async_computation | async-start | bytes 983040 | tf_op jit(solution)/shard_map/all_to_all | solution.py:97
  265.1 28.4 %all-to-all-start.2 = ((f32[64,1,1800]{2,1,0:T(1,128)}), f32[64,1,1800]{2,1,0:T(1,128)S(1)}, u32[]{:S(2)}, u32[]{:S(2)}) async-start(f32[64,1,1800]{2,1,0:T(1,128)} %reshape.487), calls=%async_computation.2 | async-start | bytes 983040 | tf_op jit(solution)/shard_map/all_to_all | solution.py:120
  319.1 5.8 %collective-permute-start.10 = (f32[1,8,45,1]{2,1,3,0:T(8,128)S(1)}, f32[1,8,45,1]{2,1,3,0:T(8,128)S(1)}, u32[]{:S(2)}, u32[]{:S(2)}) collective-permute-start(f32[1,8,45,1]{2,1,3,0:T(8,128)S(1)} %get-tuple-element.117), channel_id=1, source_target_pairs={{0,64},{64,128},{128,192},{192,0},{1,65},{65,129},{129,193},{193,1... | collective-permute-start | bytes 4328 | tf_op jit(solution)/shard_map/ppermute | solution.py:23
  319.1 6.0 %collective-permute-start.11 = (f32[1,8,45,1]{2,1,3,0:T(8,128)S(1)}, f32[1,8,45,1]{2,1,3,0:T(8,128)S(1)}, u32[]{:S(2)}, u32[]{:S(2)}) collective-permute-start(f32[1,8,45,1]{2,1,3,0:T(8,128)S(1)} %get-tuple-element.118), channel_id=1, source_target_pairs={{64,0},{128,64},{192,128},{0,192},{65,1},{129,65},{193,129},{1,193... | collective-permute-start | bytes 4328 | tf_op jit(solution)/shard_map/ppermute | solution.py:25
  322.3 10.0 %collective-permute-start.14 = (f32[1,8,45,2]{2,1,3,0:T(8,128)S(1)}, f32[1,8,45,2]{2,1,3,0:T(8,128)S(1)}, u32[]{:S(2)}, u32[]{:S(2)}) collective-permute-start(f32[1,8,45,2]{2,1,3,0:T(8,128)S(1)} %pad_maximum_fusion.30), channel_id=1, source_target_pairs={{0,32},{1,33},{2,34},{3,35},{4,36},{5,37},{6,38},{7,39},{8,40},{9,... | collective-permute-start | bytes 8648 | tf_op jit(solution)/shard_map/ppermute | solution.py:35
  325.3 8.4 %collective-permute-start.12 = (f32[1,8,1,362]{3,1,2,0:T(8,128)S(1)}, f32[1,8,1,362]{3,1,2,0:T(8,128)S(1)}, u32[]{:S(2)}, u32[]{:S(2)}) collective-permute-start(f32[1,8,1,362]{3,1,2,0:T(8,128)S(1)} %get-tuple-element.134), channel_id=1, source_target_pairs={{0,1},{1,2},{2,3},{3,4},{4,5},{5,6},{6,7},{7,8},{8,9},{9,10},{10,1... | collective-permute-start | bytes 34760 | tf_op jit(solution)/shard_map/ppermute | solution.py:23
  326.9 6.8 %collective-permute-start.13 = (f32[1,8,1,362]{3,1,2,0:T(8,128)S(1)}, f32[1,8,1,362]{3,1,2,0:T(8,128)S(1)}, u32[]{:S(2)}, u32[]{:S(2)}) collective-permute-start(f32[1,8,1,362]{3,1,2,0:T(8,128)S(1)} %get-tuple-element.135), channel_id=1, source_target_pairs={{1,0},{2,1},{3,2},{4,3},{5,4},{6,5},{7,6},{8,7},{9,8},{10,9},{11,1... | collective-permute-start | bytes 34760 | tf_op jit(solution)/shard_map/ppermute | solution.py:25
  342.5 9.5 %collective-permute-start.15 = (f32[2,8,45,1]{2,1,3,0:T(8,128)S(1)}, f32[2,8,45,1]{2,1,3,0:T(8,128)S(1)}, u32[]{:S(2)}, u32[]{:S(2)}) collective-permute-start(f32[2,8,45,1]{2,1,3,0:T(8,128)S(1)} %get-tuple-element.119), channel_id=1, source_target_pairs={{0,64},{64,128},{128,192},{192,0},{1,65},{65,129},{129,193},{193,1... | collective-permute-start | bytes 8648 | tf_op jit(solution)/shard_map/ppermute | solution.py:23
  342.6 9.7 %collective-permute-start.16 = (f32[2,8,45,1]{2,1,3,0:T(8,128)S(1)}, f32[2,8,45,1]{2,1,3,0:T(8,128)S(1)}, u32[]{:S(2)}, u32[]{:S(2)}) collective-permute-start(f32[2,8,45,1]{2,1,3,0:T(8,128)S(1)} %get-tuple-element.120), channel_id=1, source_target_pairs={{64,0},{128,64},{192,128},{0,192},{65,1},{129,65},{193,129},{1,193... | collective-permute-start | bytes 8648 | tf_op jit(solution)/shard_map/ppermute | solution.py:25
  344.3 16.8 %collective-permute-start.19 = (f32[2,8,45,2]{2,1,3,0:T(8,128)S(1)}, f32[2,8,45,2]{2,1,3,0:T(8,128)S(1)}, u32[]{:S(2)}, u32[]{:S(2)}) collective-permute-start(f32[2,8,45,2]{2,1,3,0:T(8,128)S(1)} %pad_maximum_fusion.22), channel_id=1, source_target_pairs={{0,32},{1,33},{2,34},{3,35},{4,36},{5,37},{6,38},{7,39},{8,40},{9,... | collective-permute-start | bytes 17288 | tf_op jit(solution)/shard_map/ppermute | solution.py:35
  352.0 10.7 %copy-start.8 = (f32[2,8,45,360]{3,1,2,0:T(8,128)S(1)}, f32[2,8,45,360]{3,1,2,0:T(8,128)}, u32[]{:S(2)}) copy-start(f32[2,8,45,360]{3,1,2,0:T(8,128)} %copy.170) | copy-start | bytes 3110404
  353.4 9.3 %collective-permute-start.17 = (f32[2,8,1,362]{3,1,2,0:T(8,128)S(1)}, f32[2,8,1,362]{3,1,2,0:T(8,128)S(1)}, u32[]{:S(2)}, u32[]{:S(2)}) collective-permute-start(f32[2,8,1,362]{3,1,2,0:T(8,128)S(1)} %get-tuple-element.130), channel_id=1, source_target_pairs={{0,1},{1,2},{2,3},{3,4},{4,5},{5,6},{6,7},{7,8},{8,9},{9,10},{10,1... | collective-permute-start | bytes 69512 | tf_op jit(solution)/shard_map/ppermute | solution.py:23
  355.5 7.1 %collective-permute-start.18 = (f32[2,8,1,362]{3,1,2,0:T(8,128)S(1)}, f32[2,8,1,362]{3,1,2,0:T(8,128)S(1)}, u32[]{:S(2)}, u32[]{:S(2)}) collective-permute-start(f32[2,8,1,362]{3,1,2,0:T(8,128)S(1)} %get-tuple-element.131), channel_id=1, source_target_pairs={{1,0},{2,1},{3,2},{4,3},{5,4},{6,5},{7,6},{8,7},{9,8},{10,9},{11,1... | collective-permute-start | bytes 69512 | tf_op jit(solution)/shard_map/ppermute | solution.py:25
  (7 other events, 13.6 us)
where the time goes:
time: 566 us; the launch traced here: 556 us
  other arithmetic  155 us (27%)
  local copies, waits for them, and re-layouts  123 us (22%)
  matrix products  120 us (21%)
  starting transfers between devices  81.6 us (14%)
  blocking collectives  54.1 us (10%)
  waiting for transfers between devices  21.4 us (4%)
    cos x1, other arithmetic, fourier_table(): return jnp.concatenate([jnp.cos(phase_angle), jnp.sin(phase_angle)], axis=1)  75.4 us
    dot_general x2, matrix products, filter_items(): jnp.einsum('nk,ki->ni', fourier, spectrum * weight, precision=lax.Precisi...  64.1 us
    dot_general x2, matrix products, filter_items(): jnp.einsum('nk,ni->ki', fourier, full_rows, precision=lax.Precision.HIGHE...  56.1 us
    unnamed x10, other arithmetic  55 us
    all_to_all x1, blocking collectives, filter_items(): lax.all_to_all(item_data, 'lon', split_axis=0, concat_axis=1, tiled=True)  29.9 us
    unnamed x47, local copies, waits for them, and re-layouts  26 us
    scatter x3, local copies, waits for them, and re-layouts, filter_state(): return state.at[:, :, :, chosen].set(replaced)  25.6 us
    ppermute x8, starting transfers between devices, padded_2(): lax.ppermute(head, axis, [((i + 1) % count, i) for i in range(count)])  24.9 us
  transfers between devices with their start and end apart: 23, of which 5 were waited for; matrix products, arithmetic and copies ran while one was open for 25% of the time, Pallas kernels for 0%

commit v1 on v0

v1 whole, which is shorter than its diff:
```python
import jax
import jax.numpy as jnp
import ml_dtypes
import numpy as np
from jax import lax
from jax.experimental import pallas as pl
from jax.experimental.pallas import tpu as pltpu
from jax.sharding import PartitionSpec as P

NLON, NLAT, LEV = 2880, 1440, 8
SEG, BAND, FROWS = 45, 360, 64
F32, BF16, I32 = jnp.float32, jnp.bfloat16, jnp.int32
NN = (((1,), (0,)), ((), ()))
NT = (((1,), (1,)), ((), ()))
TN = (((0,), (0,)), ((), ()))

SLOT_BASE = (0, 12, 22, 30, 38, 46, 54)
SLOT_COUNT = (12, 10, 8, 8, 8, 8, 8)
SLOT_FIRST = (-2, -1, 0, 0, 0, 0, 0)
PAIRS = 17


def slot_tables():
    rho = np.full(64, -100, np.int32)
    kind = np.full(64, -1, np.int32)
    for f, (base, count, first) in enumerate(zip(SLOT_BASE, SLOT_COUNT, SLOT_FIRST)):
        rho[base : base + count] = first + np.arange(count)
        kind[base : base + count] = f
    return rho, kind


def split_np(m):
    high = m.astype(ml_dtypes.bfloat16)
    low = (m - high.astype(np.float64)).astype(ml_dtypes.bfloat16)
    return high, low


def triple(m):
    high, low = split_np(m)
    return np.concatenate([high, low, high], axis=-1)


def fourier_constants():
    s = np.arange(64)
    k1 = np.arange(33)
    ang = 2 * np.pi * (np.outer(k1, s) % 64) / 64
    fwd = np.zeros((80, 64))
    fwd[:33], fwd[40:73] = np.cos(ang), -np.sin(ang)
    inv = np.zeros((2, 64, 2, 24))
    sig = np.zeros((PAIRS, 96, 128))
    mf = np.zeros((2 * PAIRS, 192, 48))
    mi = np.zeros((PAIRS, 192, 96))
    i, k2 = np.arange(SEG), np.arange(SEG)
    for q in range(33):
        half, pair = divmod(q, PAIRS)
        inv[half, :, 0, pair] = np.cos(ang[q])
        inv[half, :, 1, pair] = -np.sin(ang[q])
        k = q + 64 * k2
        w = 2 * np.pi * (np.outer(k, i) % NLON) / NLON
        full = np.zeros((2, 48, 2, 48))
        full[0, :SEG, 0, :SEG], full[0, :SEG, 1, :SEG] = np.cos(w), np.sin(w)
        full[1, :SEG, 0, :SEG], full[1, :SEG, 1, :SEG] = -np.sin(w), np.cos(w)
        for h in range(2):
            mf[q, 96 * h : 96 * h + 96] = full[:, :, :, 24 * h : 24 * h + 24].reshape(96, 48)
        scale = (1.0 if q in (0, 32) else 2.0) / NLON
        mi[pair, 96 * half : 96 * half + 96] = full.reshape(96, 96).T * scale
        sn = np.sin(2 * np.pi * k / NLON)
        sig[pair, :SEG, 64 * half : 64 * half + 64] = -sn[:, None]
        sig[pair, 48 : 48 + SEG, 64 * half : 64 * half + 64] = sn[:, None]
    mih, mil = split_np(mi)
    return (
        triple(fwd),
        triple(mf),
        np.concatenate([mih, mil], axis=-1),
        mih,
        triple(inv.reshape(128, 48)),
        sig.astype(np.float32),
    )


def dot(a, b, dims=NN):
    return lax.dot_general(a, b, dims, preferred_element_type=F32)


def split(x):
    high = x.astype(BF16)
    return high, (x - high.astype(F32)).astype(BF16)


def iota(shape, axis):
    return lax.broadcasted_iota(I32, shape, axis)


def edge_rows(fields, even):
    r, lane = iota((16, 384), 0), iota((16, 384), 1)
    north = (r < 2) == even
    target = jnp.where(north, BAND - 1 - r % 2, r % 2)
    pick = jnp.where((lane == target) & (r < 4), 1.0, 0.0).astype(BF16)
    high, low = split(fields)
    return dot(pick, high, NT) + dot(pick, low, NT)


def placed_rows(first_ref, second_ref, rows_ref, even, polar):
    rows_ref[...] = jnp.zeros_like(rows_ref)
    rows_ref[0:2, :] = first_ref[...]
    wind = iota((2, 1152), 1) < 768
    second = second_ref[...]
    rows_ref[2:4, :] = jnp.where(wind & polar, -second, second)
    r, lane = iota((16, 384), 0), iota((16, 384), 1)
    north = (r < 2) == even
    target = jnp.where(north, BAND + r % 2, 383 - r % 2)
    put = jnp.where((lane == target) & (r < 4), 1.0, 0.0).astype(BF16)
    high, low = split(rows_ref[...])
    return dot(high, put, TN) + dot(low, put, TN)


def lat_of(ids_ref):
    b = ids_ref[0]
    return b, b % 2 == 0, (b == 0) | (b == 3)


def shift_lanes(x, by):
    return pltpu.roll(x, by % x.shape[-1], x.ndim - 1)


def edges_kernel(ids_ref, u_ref, v_ref, p_ref, east_ref, west_ref, first_ref, second_ref, box_ref):
    _, even, _ = lat_of(ids_ref)
    box_ref[...] = jnp.zeros_like(box_ref)
    for f, ref in enumerate((u_ref, v_ref, p_ref)):
        box_ref[f, :, 0:SEG, 0:BAND] = ref[0]
    send_edges(box_ref, (0, 1, 2), even, east_ref, west_ref, first_ref, second_ref)


def send_edges(box_ref, uvp, even, east_ref, west_ref, first_ref, second_ref):
    u, v, p = uvp
    for slot, (f, col) in enumerate(((p, 43), (p, 44), (u, 44), (v, 44))):
        east_ref[slot] = box_ref[f, :, col, :]
    for slot, (f, col) in enumerate(((p, 1), (p, 0), (u, 0), (v, 0))):
        west_ref[slot] = box_ref[f, :, col, :]
    fields = jnp.concatenate([box_ref[f].reshape(384, 384) for f in uvp], axis=0)
    rows = edge_rows(fields, even)
    first_ref[...] = rows[0:2]
    second_ref[...] = rows[2:4]


def fill_columns(ext_ref, from_west_ref, from_east_ref):
    ext_ref[2, :, 6, :] = from_west_ref[0]
    ext_ref[2, :, 7, :] = from_west_ref[1]
    ext_ref[0, :, 7, :] = from_west_ref[2]
    ext_ref[1, :, 7, :] = from_west_ref[3]
    ext_ref[2, :, 54, :] = from_east_ref[0]
    ext_ref[2, :, 53, :] = from_east_ref[1]
    ext_ref[0, :, 53, :] = from_east_ref[2]
    ext_ref[1, :, 53, :] = from_east_ref[3]


def first_kernel(
    ids_ref, state_ref, from_west_ref, from_east_ref, got_first_ref, got_second_ref, tab_ref,
    out_ref, east_ref, west_ref, first_ref, second_ref, ext_ref, rows_ref, w_ref,
):
    _, even, polar = lat_of(ids_ref)
    placed = placed_rows(got_first_ref, got_second_ref, rows_ref, even, polar)
    ext_ref[...] = jnp.zeros_like(ext_ref)
    ext_ref[:, :, 8:56, :] = placed.reshape(3, LEV, 48, 384)
    for f, field in enumerate((0, 1, 3)):
        ext_ref[f, :, 8 : 8 + SEG, 0:BAND] = state_ref[field]
    fill_columns(ext_ref, from_west_ref, from_east_ref)
    a, f, c, qc = (tab_ref[n : n + 1, :] for n in range(4))
    w_ref[...] = jnp.zeros_like(w_ref)
    for lev in range(LEV):
        new_w = state_ref[2, lev] + 0.3 * state_ref[4, lev]
        if lev + 1 < LEV:
            new_w -= 0.25 * state_ref[3, lev + 1]
        if lev > 0:
            new_w += 0.25 * state_ref[3, lev - 1]
        w_ref[lev, 0:SEG, 0:BAND] = new_w
    keep = (iota((48, 384), 0) < SEG) & (iota((48, 384), 1) < BAND)
    for lev in range(LEV):
        u = ext_ref[0, lev, 7:55, :]
        v = ext_ref[1, lev, 7:55, :]
        new_u = u - (0.5 * a) * (ext_ref[2, lev, 8:56, :] - ext_ref[2, lev, 6:54, :]) + f * v
        ext_ref[0, lev, 7:55, :] = new_u
        uc = (u, v)
        del uc
        p = ext_ref[2, lev, 8:56, :]
        old_v = ext_ref[1, lev, 8:56, :]
        old_u = u[1:, :]
        old_u = jnp.concatenate([old_u, u[0:1, :]], axis=0)
        new_v = old_v - 0.25 * (shift_lanes(p, -1) - shift_lanes(p, 1)) - f * old_u
        flux = c * new_v
        new_p = p - (0.5 * a) * (ext_ref[0, lev, 9:57, :] - ext_ref[0, lev, 7:55, :])
        new_p -= qc * (shift_lanes(flux, -1) - shift_lanes(flux, 1))
        if lev + 1 < LEV:
            new_p -= 0.25 * w_ref[lev + 1]
        if lev > 0:
            new_p += 0.25 * w_ref[lev - 1]
        out_ref[0, lev] = jnp.where(keep, ext_ref[0, lev, 8:56, :], 0.0)
        out_ref[1, lev] = jnp.where(keep, new_v, 0.0)
        out_ref[2, lev] = w_ref[lev]
        out_ref[3, lev] = jnp.where(keep, new_p, 0.0)
        out_ref[4, lev] = jnp.zeros((48, 384), F32)
        out_ref[4, lev, 0:SEG, 0:BAND] = state_ref[4, lev] - 0.3 * w_ref[lev, 0:SEG, 0:BAND]
    send_edges(out_ref, (0, 1, 3), even, east_ref, west_ref, first_ref, second_ref)


def row_lanes(ids_ref, rows_ref, index):
    b = ids_ref[0]
    at = jnp.where(b >= 2, FROWS, 0)
    lane = jnp.full(index.shape, -1, I32)
    for k in range(FROWS):
        e = rows_ref[at + k] - BAND * b
        e = jnp.where(e < 0, jnp.where(e >= -2, e + 384, -1), jnp.where(e <= BAND + 1, e, -1))
        lane = jnp.where(index == k, e, lane)
    return lane


def pack_kernel(
    ids_ref, rows_ref, r_ref, got_first_ref, got_second_ref, tab_ref, slot_ref,
    out_ref, next_ref, x_ref, edge_ref,
):
    _, even, polar = lat_of(ids_ref)
    placed = placed_rows(got_first_ref, got_second_ref, edge_ref, even, polar).reshape(3, LEV, 48, 384)
    a, f, c, qc = (tab_ref[n : n + 1, :] for n in range(4))
    for lev in range(LEV):
        new_w = r_ref[2, lev] + 0.3 * r_ref[4, lev]
        if lev + 1 < LEV:
            new_w -= 0.25 * r_ref[3, lev + 1]
        if lev > 0:
            new_w += 0.25 * r_ref[3, lev - 1]
        next_ref[1, lev] = new_w
    for lev in range(LEV):
        u = r_ref[0, lev] + placed[0, lev]
        v = r_ref[1, lev] + placed[1, lev]
        p = r_ref[3, lev] + placed[2, lev]
        g = v - f * u
        new_v = g - 0.25 * (shift_lanes(p, -1) - shift_lanes(p, 1))
        flux = c * new_v
        new_p = p - qc * (shift_lanes(flux, -1) - shift_lanes(flux, 1))
        if lev + 1 < LEV:
            new_p -= 0.25 * next_ref[1, lev + 1]
        if lev > 0:
            new_p += 0.25 * next_ref[1, lev - 1]
        new_w = next_ref[1, lev]
        new_t = r_ref[4, lev] - 0.3 * new_w
        next_ref[0, lev] = new_v
        next_ref[2, lev] = new_p
        next_ref[3, lev] = new_t
        at = pl.ds(48 * lev, 48)
        for n, value in enumerate((p, g, u + f * v, new_v, new_w, new_p, new_t)):
            high, low = split(value)
            x_ref[0, at, 384 * n : 384 * n + 384] = high
            x_ref[1, at, 384 * n : 384 * n + 384] = low
    lane = row_lanes(ids_ref, rows_ref, slot_ref[0:1, :])
    kind = slot_ref[1:2, :]
    row = iota((384, 512), 0)
    one_hot = jnp.concatenate(
        [jnp.where(row == jnp.where(kind == n, lane, -1), 1.0, 0.0).astype(BF16) for n in range(7)],
        axis=0,
    )
    got = dot(x_ref[0], one_hot) + dot(x_ref[1], one_hot)
    low_half = iota((24, 128), 1) < 64
    for lev in range(LEV):
        for t in range(4):
            tile = got[48 * lev : 48 * lev + 48, 128 * t : 128 * t + 128]
            top, bottom = tile[0:24], tile[24:48]
            out_ref[8 * lev + 2 * t] = jnp.where(low_half, top, shift_lanes(bottom, 64))
            out_ref[8 * lev + 2 * t + 1] = jnp.where(low_half, shift_lanes(top, 64), bottom)


def zonal_kernel(r_ref, p2_ref, from_west_ref, from_east_ref, tab_ref, out_ref, ext_ref):
    a, f = tab_ref[0:1, :], tab_ref[1:2, :]
    ext_ref[:, :, 0:8, :] = jnp.zeros((3, LEV, 8, 384), F32)
    ext_ref[:, :, 56:64, :] = jnp.zeros((3, LEV, 8, 384), F32)
    for n, field in enumerate((0, 1, 3)):
        ext_ref[n, :, 8:56, :] = r_ref[field]
    fill_columns(ext_ref, from_west_ref, from_east_ref)
    for lev in range(LEV):
        new_u = (
            ext_ref[0, lev, 7:55, :]
            - (0.5 * a) * (ext_ref[2, lev, 8:56, :] - ext_ref[2, lev, 6:54, :])
            + f * ext_ref[1, lev, 7:55, :]
        )
        ext_ref[0, lev, 7:55, :] = new_u
        out_ref[0, lev] = ext_ref[0, lev, 8:56, :]
        out_ref[1, lev] = p2_ref[2, lev] - (0.5 * a) * (
            ext_ref[0, lev, 9:57, :] - ext_ref[0, lev, 7:55, :]
        )


def spectral_kernel(
    ids_ref, rows_ref, cut_ref, cos_ref, in_ref, slot_ref, fwd_ref, mf_ref, mi2_ref, mi1_ref, inv_ref, sig_ref,
    out_ref, z_ref, y_ref, mix_ref,
):
    b, owner = ids_ref[0], ids_ref[1]
    at = jnp.where(b >= 2, FROWS, 0)
    first = 8 * (owner % 8)
    low_half = iota((96, 128), 1) < 64
    for r in range(0, 24, 2):
        high0, low0 = split(in_ref[:, r, :])
        high1, low1 = split(in_ref[:, r + 1, :])
        both = jnp.concatenate(
            [
                jnp.concatenate([high0, high0, low0], axis=0),
                jnp.concatenate([high1, high1, low1], axis=0),
            ],
            axis=1,
        )
        z = dot(fwd_ref[...], both)
        for n in range(2):
            part = z[:, 128 * n : 128 * n + 128]
            z_ref[:, r + n, :] = part[0:40]
            z_ref[:, 24 + r + n, :] = part[40:80]
    rho = slot_ref[2:3, 0:128]
    kind = slot_ref[3:4, 0:128]

    def listed(k):
        return jnp.where((k >= 0) & (k < FROWS), rows_ref[at + jnp.clip(k, 0, FROWS - 1)], -1000)

    row_at = [listed(first + t) for t in range(-4, 12)]
    cut_at = [cut_ref[at + jnp.clip(first + t, 0, FROWS - 1)] for t in range(-4, 12)]
    blank = jnp.zeros((1, 128), F32)
    rows = [jnp.full((1, 128), -1000, I32) for _ in range(5)]
    cut, c0, cp, cm = jnp.zeros((1, 128), I32), blank + 1.0, blank, blank
    for t in range(-2, 10):
        here = rho == t
        j = row_at[t + 4]
        jc = jnp.clip(j, 0, NLAT - 1)
        for d in range(-2, 3):
            rows[d + 2] = jnp.where(here, row_at[t + d + 4], rows[d + 2]) if 0 <= t + d + 4 < 16 else rows[d + 2]
        cut = jnp.where(here, cut_at[t + 4], cut)
        cm = jnp.where(here, cos_ref[jc], cm)
        c0 = jnp.where(here, cos_ref[jc + 1], c0)
        cp = jnp.where(here, cos_ref[jc + 2], cp)
    j = rows[2]

    def yes(cond):
        return jnp.where(cond, 1.0, 0.0)

    up1, dn1 = yes(rows[3] == j + 1), yes(rows[1] == j - 1)
    up2, up22 = yes(rows[3] == j + 2), yes(rows[4] == j + 2)
    dn2, dn22 = yes(rows[1] == j - 2), yes(rows[0] == j - 2)
    south, north = yes(j == 0), yes(j == NLAT - 1)
    a = 0.5 * cos_ref[1] / c0
    qc = -0.25 / c0
    src, dst = iota((128, 128), 0), iota((128, 128), 1)

    def mix(terms):
        total = jnp.zeros((128, 128), F32)
        for to, shift, coef in terms:
            total = jnp.where(src == dst - shift, jnp.where(kind == to, coef, 0.0), total) if False else (
                total + jnp.where((src == dst - shift) & (kind == to), coef, 0.0)
            )
        return total

    on_d = mix([(2, 20, -a), (5, 24, -a)])
    on_s = mix([(5, 44, -a * a)])
    q0 = -0.25 * (cp * (1 - north) + cm * (1 - south) + c0 * (south + north))
    on_h = mix(
        [
            (1, 10, 0.25 * up1), (1, 12, -0.25 * dn1),
            (3, 27, 0.25 * up1), (3, 29, -0.25 * dn1), (3, 17, blank - 1.0),
            (5, 44, qc * q0),
            (5, 43, qc * 0.25 * cp * up2), (5, 42, qc * 0.25 * cp * up22),
            (5, 45, qc * 0.25 * cm * dn2), (5, 46, qc * 0.25 * cm * dn22),
            (5, 32, -qc * cp * up1), (5, 34, qc * cm * dn1),
        ]
    )
    pole = 0.25 * (north - south)
    on_p = mix(
        [
            (1, 11, pole), (3, 28, pole),
            (5, 43, qc * 0.25 * (cp * yes(j == NLAT - 2) + c0 * south * up1)),
            (5, 45, qc * 0.25 * (cm * yes(j == 1) + c0 * north * dn1)),
            (5, 33, qc * c0 * (north - south)),
        ]
    )
    for n, m in enumerate((on_d, on_s, on_h, on_p)):
        high, low = split(m)
        mix_ref[0, 128 * n : 128 * n + 128, :] = high
        mix_ref[1, 128 * n : 128 * n + 128, :] = low
    final = kind >= 2
    sign = jnp.where(kind == 1, -1.0, 1.0)
    k_base = 64 * (iota((96, 128), 0) % 48) + jnp.where(low_half, 0, PAIRS)
    odd_base = jnp.where(iota((96, 128), 1) < 64, 1.0, -1.0)
    y_ref[PAIRS:24] = jnp.zeros((24 - PAIRS, 96, 128), F32)
    for pair in range(PAIRS):
        parts = []
        for half in range(2):
            q = pair + PAIRS * half
            high, low = split(z_ref[q])
            got = dot(mf_ref[q], jnp.concatenate([high, high, low], axis=0))
            parts.append(got)
        s = jnp.where(
            low_half,
            parts[0][0:96] + shift_lanes(parts[0][96:192], 64),
            shift_lanes(parts[1][0:96], 64) + parts[1][96:192],
        )
        k = k_base + pair
        keep = jnp.minimum(k, NLON - k) <= cut
        h = jnp.where(keep, 0.0, s)
        sig = sig_ref[pair]
        d = sig * jnp.concatenate([s[48:96], s[0:48]], axis=0)
        ph = (odd_base if pair % 2 == 0 else -odd_base) * h
        terms = jnp.concatenate([d, sig * sig * s, h, ph], axis=1)
        high, low = split(terms)
        corr = dot(high, mix_ref[0]) + dot(low, mix_ref[0]) + dot(high, mix_ref[1])
        t = jnp.where(final, jnp.where(keep, s + corr, 0.0), sign * h + corr)
        high, low = split(t)
        back = dot(mi2_ref[pair], jnp.concatenate([high, high], axis=0)) + dot(mi1_ref[pair], low)
        y_ref[pair] = jnp.where(low_half, back[0:96], back[96:192])
    half64 = iota((64, 128), 1) < 64
    for r in range(24):
        cols = []
        for i in (r, r + 24):
            zz = jnp.concatenate([y_ref[:, i, :], y_ref[:, 48 + i, :]], axis=0)
            high, low = split(zz)
            cols.append(jnp.concatenate([high, high, low], axis=0))
        x = dot(inv_ref[...], jnp.concatenate(cols, axis=1))
        out_ref[:, r, :] = jnp.where(
            half64,
            x[0:64, 0:128] + shift_lanes(x[64:128, 0:128], 64),
            shift_lanes(x[0:64, 128:256], 64) + x[64:128, 128:256],
        )


def final_kernel(ids_ref, rows_ref, in_ref, next_ref, zonal_ref, tab_ref, slot_ref, out_ref, b_ref):
    low_half = iota((24, 128), 1) < 64
    for lev in range(LEV):
        for t in range(4):
            even, odd = in_ref[8 * lev + 2 * t], in_ref[8 * lev + 2 * t + 1]
            tile = jnp.concatenate(
                [
                    jnp.where(low_half, even, shift_lanes(odd, 64)),
                    jnp.where(low_half, shift_lanes(even, 64), odd),
                ],
                axis=0,
            )
            high, low = split(tile)
            b_ref[0, 48 * lev : 48 * lev + 48, 128 * t : 128 * t + 128] = high
            b_ref[1, 48 * lev : 48 * lev + 48, 128 * t : 128 * t + 128] = low
    index = slot_ref[0:1, :]
    rho = slot_ref[2:3, :]
    own = (rho >= 0) & (rho < 8)
    lane = row_lanes(ids_ref, rows_ref, index)
    kind = slot_ref[1:2, :]
    row = iota((384, 512), 0)

    def spread(n):
        one_hot = jnp.where(row == jnp.where((kind == n) & own, lane, -1), 1.0, 0.0).astype(BF16)
        return dot(b_ref[0], one_hot, NT) + dot(b_ref[1], one_hot, NT)

    flag = jnp.zeros((1, 384), F32)
    at = jnp.where(ids_ref[0] >= 2, FROWS, 0)
    lanes = iota((1, 384), 1)
    for k in range(FROWS):
        e = rows_ref[at + k] - BAND * ids_ref[0]
        e = jnp.where((e < 0) & (e >= -2), e + 384, e)
        flag = jnp.where(lanes == e, 1.0, flag)
    flagged = flag > 0.5
    inner = flagged[:, 0:BAND]
    c, qc = tab_ref[2:3, :], tab_ref[3:4, :]
    hp, dv = spread(0), spread(1)
    dv = jnp.where(flagged, dv, 0.25 * (shift_lanes(hp, -1) - shift_lanes(hp, 1)))
    flux = c * dv
    dp = -qc * (shift_lanes(flux, -1) - shift_lanes(flux, 1))
    sources = (
        (0, 2, lambda lev: zonal_ref[0, lev]),
        (1, 3, lambda lev: next_ref[0, lev] + dv[48 * lev : 48 * lev + 48]),
        (2, 4, lambda lev: next_ref[1, lev]),
        (3, 5, lambda lev: zonal_ref[1, lev] + dp[48 * lev : 48 * lev + 48]),
        (4, 6, lambda lev: next_ref[3, lev]),
    )
    for field, n, plain in sources:
        filtered = spread(n)
        for lev in range(LEV):
            out_ref[field, lev] = jnp.where(
                inner, filtered[48 * lev : 48 * lev + SEG, 0:BAND], plain(lev)[0:SEG, 0:BAND]
            )


VMEM = pl.BlockSpec(memory_space=pltpu.VMEM)
SMEM = pl.BlockSpec(memory_space=pltpu.SMEM)


def call(body, name, n_smem, args, outs, scratch, flops, mib):
    return pl.pallas_call(
        body,
        name=name,
        out_shape=outs,
        in_specs=[SMEM] * n_smem + [VMEM] * (len(args) - n_smem),
        out_specs=jax.tree.map(lambda _: VMEM, outs),
        scratch_shapes=scratch,
        compiler_params=pltpu.CompilerParams(vmem_limit_bytes=mib << 20),
        cost_estimate=pl.CostEstimate(flops=flops, bytes_accessed=8 << 20, transcendentals=0),
    )(*args)


def shape(*dims):
    return jax.ShapeDtypeStruct(dims, F32)


def neighbours():
    first, second = [], []
    for l in range(64):
        for b in (0, 2):
            first += [(64 * b + l, 64 * b + 64 + l), (64 * b + 64 + l, 64 * b + l)]
        second += [(64 + l, 128 + l), (128 + l, 64 + l)]
        second += [(l, (l + 32) % 64), (192 + l, 192 + (l + 32) % 64)]
    return first, second


def exchange(edges):
    east, west, first, second = edges
    pairs_first, pairs_second = neighbours()
    got_first = lax.ppermute(first, ("lat", "lon"), pairs_first)
    got_second = lax.ppermute(second, ("lat", "lon"), pairs_second)
    from_west = lax.ppermute(east, "lon", [(i, (i + 1) % 64) for i in range(64)])
    from_east = lax.ppermute(west, "lon", [((i + 1) % 64, i) for i in range(64)])
    return from_west, from_east, got_first, got_second


def row_tables(b):
    def cosine(row):
        return jnp.abs(jnp.sin((row.astype(F32) + 0.5) * (jnp.pi / NLAT)))

    lane = jnp.arange(384, dtype=I32)
    row = jnp.where(lane < 370, lane, lane - 384) + BAND * b
    c = cosine(row)
    f = -0.2 * jnp.cos((row.astype(F32) + 0.5) * (jnp.pi / NLAT))
    polar = cosine(jnp.zeros((), I32))
    zero = jnp.zeros_like(c)
    tab = jnp.stack([0.5 * polar / c, f, c, 0.25 / c, zero, zero, zero, zero])
    return tab, cosine(jnp.arange(-1, 1447, dtype=I32))


def per_device(prognostic, filter_rows, cutoff):
    b, lon = lax.axis_index("lat"), lax.axis_index("lon")
    ids = jnp.stack([b, lon]).astype(I32)
    tab, cosines = row_tables(b)
    rho64, kind64 = slot_tables()
    slots = np.full((8, 512), -1, np.int32)
    slots[0] = (8 * np.arange(8)[:, None] + rho64[None, :]).reshape(-1)
    slots[1] = np.tile(kind64, 8)
    slots[2] = np.tile(rho64, 8)
    slots[3] = np.tile(kind64, 8)
    margin = (slots[2] < 0) | (slots[2] > 7)
    slots[3] = np.where(margin & (slots[1] == 1), 0, slots[3])
    slots = jnp.asarray(slots)
    fwd, mf, mi2, mi1, inv, sig = (jnp.asarray(x) for x in fourier_constants())

    edge_shapes = (shape(4, 8, 384), shape(4, 8, 384), shape(2, 1152), shape(2, 1152))
    winds = [prognostic[n : n + 1] for n in (0, 1, 3)]
    edges = call(
        edges_kernel, "edges", 1, (ids, *winds), edge_shapes,
        [pltpu.VMEM((3, 8, 48, 384), F32)], 10**7, 16,
    )
    state, *edges = call(
        first_kernel, "first", 1, (ids, prognostic, *exchange(edges), tab),
        (shape(5, 8, 48, 384), *edge_shapes),
        [pltpu.VMEM((3, 8, 64, 384), F32), pltpu.VMEM((16, 1152), F32), pltpu.VMEM((8, 48, 384), F32)],
        10**8, 24,
    )
    from_west, from_east, got_first, got_second = exchange(edges)
    message, after = call(
        pack_kernel, "pack", 2,
        (ids, filter_rows, state, got_first, got_second, tab, slots),
        (shape(64, 24, 128), shape(4, 8, 48, 384)),
        [pltpu.VMEM((2, 384, 2688), BF16), pltpu.VMEM((16, 1152), F32)], 10**9, 32,
    )
    whole = lax.all_to_all(message, "lon", split_axis=0, concat_axis=0, tiled=True)
    zonal = call(
        zonal_kernel, "zonal", 0, (state, after, from_west, from_east, tab),
        shape(2, 8, 48, 384), [pltpu.VMEM((3, 8, 64, 384), F32)], 10**8, 16,
    )
    answer = call(
        spectral_kernel, "spectral", 4,
        (ids, filter_rows, cutoff, cosines, whole, slots, fwd, mf, mi2, mi1, inv, sig),
        shape(64, 24, 128),
        [pltpu.VMEM((40, 48, 128), F32), pltpu.VMEM((24, 96, 128), F32), pltpu.VMEM((2, 512, 128), BF16)],
        10**9, 24,
    )
    back = lax.all_to_all(answer, "lon", split_axis=0, concat_axis=0, tiled=True)
    return call(
        final_kernel, "final", 2, (ids, filter_rows, back, after, zonal, tab, slots),
        shape(5, 8, 45, 360), [pltpu.VMEM((2, 384, 512), BF16)], 10**9, 32,
    )


def solution(mesh):
    in_specs = (P(None, None, "lon", "lat"), P(), P())
    out_specs = P(None, None, "lon", "lat")
    return jax.shard_map(
        per_device, mesh=mesh, in_specs=in_specs, out_specs=out_specs, check_vma=False
    )
```

time: 566 us -> 129 us (0.23)
  the two profiles are of different devices: /device:TPU:8 before, /device:TPU:2 now
where the time goes in v1:
time: 129 us; the launch traced here: 128 us
  waiting for transfers between devices  46 us (36%)
  starting transfers between devices  37.4 us (29%)
  Pallas kernels  28.4 us (22%)
  local copies, waits for them, and re-layouts  16.2 us (13%)
    pallas_call x6, Pallas kernels, call(): pl.pallas_call(body, name=name, out_shape=outs, in_specs=[SMEM] * n_smem...  28.4 us
    all_to_all x1, waiting for transfers between devices, per_device(): lax.all_to_all(message, 'lon', split_axis=0, concat_axis=0, tiled=True)  26.1 us
    ppermute x2, waiting for transfers between devices, exchange(): lax.ppermute(east, 'lon', [(i, (i + 1) % 64) for i in range(64)])  17.2 us
    unnamed x29, local copies, waits for them, and re-layouts  13.7 us
    ppermute x2, starting transfers between devices, exchange(): lax.ppermute(west, 'lon', [((i + 1) % 64, i) for i in range(64)])  12.7 us
    all_to_all x1, starting transfers between devices, per_device(): lax.all_to_all(message, 'lon', split_axis=0, concat_axis=0, tiled=True)  8.08 us
    all_to_all x1, starting transfers between devices, per_device(): lax.all_to_all(answer, 'lon', split_axis=0, concat_axis=0, tiled=True)  6.12 us
    ppermute x2, starting transfers between devices, exchange(): lax.ppermute(east, 'lon', [(i, (i + 1) % 64) for i in range(64)])  5.24 us
  transfers between devices with their start and end apart: 10, of which 4 were waited for; matrix products, arithmetic and copies ran while one was open for 0% of the time, Pallas kernels for 0%

profile of v1, /device:TPU:2, one launch (start us, length us, event | category | flops | bytes accessed | tf_op | source)
XLA Modules:
  0.0 128.5 jit_solution(5370230690300328928)
XLA Ops:
  0.0 2.3 %copy.14.state_ref = f32[5,8,45,360]{3,2,1,0:T(8,128)S(1)} copy(f32[5,8,45,360]{3,1,2,0:T(8,128)} %param.10) | data formatting | bytes 5184000 | tf_op args[0]
  2.3 0.1 fusion.4
  2.5 0.1 pad_add_fusion.ids_ref
  2.6 1.2 edges.1
  3.8 2.2 %collective-permute-start = (f32[4,8,384]{2,1,0:T(8,128)S(1)}, f32[4,8,384]{2,1,0:T(8,128)S(1)}, u32[]{:S(2)}, u32[]{:S(2)}) collective-permute-start(f32[4,8,384]{2,1,0:T(8,128)S(1)} %get-tuple-element.16), channel_id=1, source_target_pairs={{0,1},{1,2},{2,3},{3,4},{4,5},{5,6},{6,7},{7,8},{8,9},{9,10},{10,1... | collective-permute-start | bytes 147464 | tf_op jit(solution)/shard_map/ppermute | solution.py:517
  5.9 7.8 %collective-permute-start.1 = (f32[4,8,384]{2,1,0:T(8,128)S(1)}, f32[4,8,384]{2,1,0:T(8,128)S(1)}, u32[]{:S(2)}, u32[]{:S(2)}) collective-permute-start(f32[4,8,384]{2,1,0:T(8,128)S(1)} %get-tuple-element.17), channel_id=1, source_target_pairs={{1,0},{2,1},{3,2},{4,3},{5,4},{6,5},{7,6},{8,7},{9,8},{10,9},{11,1... | collective-permute-start | bytes 147464 | tf_op jit(solution)/shard_map/ppermute | solution.py:518
  13.8 1.5 %collective-permute-start.3 = (f32[2,1152]{1,0:T(2,128)S(1)}, f32[2,1152]{1,0:T(2,128)S(1)}, u32[]{:S(2)}, u32[]{:S(2)}) collective-permute-start(f32[2,1152]{1,0:T(2,128)S(1)} %get-tuple-element.19), channel_id=1, source_target_pairs={{64,128},{128,64},{0,32},{192,224},{65,129},{129,65},{1,33},{193,2... | collective-permute-start | bytes 27656 | tf_op jit(solution)/shard_map/ppermute | solution.py:516
  15.5 1.4 %collective-permute-done.3.got_second_ref = f32[2,1152]{1,0:T(2,128)S(1)} collective-permute-done((f32[2,1152]{1,0:T(2,128)S(1)}, f32[2,1152]{1,0:T(2,128)S(1)}, u32[]{:S(2)}, u32[]{:S(2)}) %collective-permute-start.3) | collective-permute-done | bytes 9248 | tf_op jit(solution)/shard_map/ppermute | solution.py:516
  16.9 2.8 %first.1 = (f32[5,8,48,384]{3,2,1,0:T(8,128)S(1)}, f32[4,8,384]{2,1,0:T(8,128)S(1)}, f32[4,8,384]{2,1,0:T(8,128)S(1)}, f32[2,1152]{1,0:T(2,128)S(1)}, f32[2,1152]{1,0:T(2,128)S(1)}) custom-call(s32[2]{0:T(128)S(1)} %pad_add_fusion.ids_ref, f32[5,8,45,360]{3,2,1,0:T(8,128)S(1)} %copy.14.state_ref, f32[4,8,384]{2,1,0:T(8,128)S(1)} %collective-permute-done.from_west_ref, ...), custom_call_target="tpu_custom_call" | custom-call | flops 100000000 | bytes 8388608 | tf_op jit(solution)/shard_map/first/pallas_call | solution.py:486
  19.7 1.5 %collective-permute-start.4 = (f32[2,1152]{1,0:T(2,128)S(1)}, f32[2,1152]{1,0:T(2,128)S(1)}, u32[]{:S(2)}, u32[]{:S(2)}) collective-permute-start(f32[2,1152]{1,0:T(2,128)S(1)} %get-tuple-element.21), channel_id=1, source_target_pairs={{0,64},{64,0},{128,192},{192,128},{1,65},{65,1},{129,193},{193,129... | collective-permute-start | bytes 27656 | tf_op jit(solution)/shard_map/ppermute | solution.py:515
  21.2 2.2 %collective-permute-start.5 = (f32[2,1152]{1,0:T(2,128)S(1)}, f32[2,1152]{1,0:T(2,128)S(1)}, u32[]{:S(2)}, u32[]{:S(2)}) collective-permute-start(f32[2,1152]{1,0:T(2,128)S(1)} %get-tuple-element.22), channel_id=1, source_target_pairs={{64,128},{128,64},{0,32},{192,224},{65,129},{129,65},{1,33},{193,2... | collective-permute-start | bytes 27656 | tf_op jit(solution)/shard_map/ppermute | solution.py:516
  23.4 1.4 %collective-permute-done.5.got_second_ref = f32[2,1152]{1,0:T(2,128)S(1)} collective-permute-done((f32[2,1152]{1,0:T(2,128)S(1)}, f32[2,1152]{1,0:T(2,128)S(1)}, u32[]{:S(2)}, u32[]{:S(2)}) %collective-permute-start.5) | collective-permute-done | bytes 9248 | tf_op jit(solution)/shard_map/ppermute | solution.py:516
  24.8 4.6 %pack.1 = (f32[64,24,128]{2,1,0:T(8,128)S(1)}, f32[4,8,48,384]{3,2,1,0:T(8,128)S(1)}) custom-call(s32[2]{0:T(128)S(1)} %pad_add_fusion.ids_ref, s32[128]{0:T(128)S(1)} %copy-done.11, f32[5,8,48,384]{3,2,1,0:T(8,128)S(1)} %get-tuple-element.20.r_ref, f32[2,1152]{1,0:T(2,128)S(1)} %collective-permute-done.4.got_first_ref, ...), custom_call_target="tpu_custom_call" | custom-call | flops 1000000000 | bytes 8388608 | tf_op jit(solution)/shard_map/pack/pallas_call | solution.py:486
  29.4 1.6 %copy-done.1 = f32[5,8,48,384]{3,2,1,0:T(8,128)} copy-done((f32[5,8,48,384]{3,2,1,0:T(8,128)}, f32[5,8,48,384]{3,2,1,0:T(8,128)S(1)}, u32[]{:S(2)}) %copy-start.1) | copy-done | bytes 2949144
  31.0 0.9 copy-done.6
  31.9 8.1 %all-to-all-start = ((f32[64,24,128]{2,1,0:T(8,128)}), f32[64,24,128]{2,1,0:T(8,128)S(1)}, u32[]{:S(2)}, u32[]{:S(2)}) async-start(f32[64,24,128]{2,1,0:T(8,128)} %copy-done.6), calls=%async_computation | async-start | bytes 1572864 | tf_op jit(solution)/shard_map/all_to_all | solution.py:570
  40.0 26.1 %all-to-all-done.in_ref = f32[64,24,128]{2,1,0:T(8,128)S(1)} async-done(((f32[64,24,128]{2,1,0:T(8,128)}), f32[64,24,128]{2,1,0:T(8,128)S(1)}, u32[]{:S(2)}, u32[]{:S(2)}) %all-to-all-start) | async-done | bytes 786464 | tf_op jit(solution)/shard_map/all_to_all | solution.py:570
  66.1 1.9 %copy-done = bf16[34,192,144]{2,1,0:T(8,128)(2,1)S(1)} copy-done((bf16[34,192,144]{2,1,0:T(8,128)(2,1)S(1)}, bf16[34,192,144]{2,1,0:T(8,128)(2,1)}, u32[]{:S(2)}) %copy-start) | copy-done | bytes 1880088
  68.0 1.4 %copy-done.3 = bf16[17,192,192]{2,1,0:T(8,128)(2,1)S(1)} copy-done((bf16[17,192,192]{2,1,0:T(8,128)(2,1)S(1)}, bf16[17,192,192]{2,1,0:T(8,128)(2,1)}, u32[]{:S(2)}) %copy-start.3) | copy-done | bytes 1253400
  69.5 1.1 copy-done.4
  70.6 1.1 copy-done.5
  71.8 14.6 %spectral.1 = f32[64,24,128]{2,1,0:T(8,128)} custom-call(s32[2]{0:T(128)S(1)} %pad_add_fusion.ids_ref, s32[128]{0:T(128)S(1)} %copy-done.11, s32[128]{0:T(128)S(1)} %copy-done.13, f32[1448]{0:T(1024)S(1)} %sine_abs_fusion.cos_ref, f32[64,24,128]{2,1,0:T(8,128)S(1)} %all-to-all-done.in_ref, s32[8,512]{1,0:T(8,128)S(1)} %copy-done.8, ...), custom_call_target="tpu_custom_call" | custom-call | flops 1000000000 | bytes 8388608 | tf_op jit(solution)/shard_map/spectral/pallas_call | solution.py:486
  86.4 6.1 %all-to-all-start.1 = ((f32[64,24,128]{2,1,0:T(8,128)}), f32[64,24,128]{2,1,0:T(8,128)}, u32[]{:S(2)}, u32[]{:S(2)}) async-start(f32[64,24,128]{2,1,0:T(8,128)} %spectral.1), calls=%async_computation.1 | async-start | bytes 1572864 | tf_op jit(solution)/shard_map/all_to_all | solution.py:582
  92.5 3.1 %collective-permute-start.6 = (f32[4,8,384]{2,1,0:T(8,128)S(1)}, f32[4,8,384]{2,1,0:T(8,128)S(1)}, u32[]{:S(2)}, u32[]{:S(2)}) collective-permute-start(f32[4,8,384]{2,1,0:T(8,128)S(1)} %get-tuple-element.25), channel_id=1, source_target_pairs={{0,1},{1,2},{2,3},{3,4},{4,5},{5,6},{6,7},{7,8},{8,9},{9,10},{10,1... | collective-permute-start | bytes 147464 | tf_op jit(solution)/shard_map/ppermute | solution.py:517
  95.6 4.8 %collective-permute-start.7 = (f32[4,8,384]{2,1,0:T(8,128)S(1)}, f32[4,8,384]{2,1,0:T(8,128)S(1)}, u32[]{:S(2)}, u32[]{:S(2)}) collective-permute-start(f32[4,8,384]{2,1,0:T(8,128)S(1)} %get-tuple-element.26), channel_id=1, source_target_pairs={{1,0},{2,1},{3,2},{4,3},{5,4},{6,5},{7,6},{8,7},{9,8},{10,9},{11,1... | collective-permute-start | bytes 147464 | tf_op jit(solution)/shard_map/ppermute | solution.py:518
  100.4 17.2 %collective-permute-done.6.from_west_ref = f32[4,8,384]{2,1,0:T(8,128)S(1)} collective-permute-done((f32[4,8,384]{2,1,0:T(8,128)S(1)}, f32[4,8,384]{2,1,0:T(8,128)S(1)}, u32[]{:S(2)}, u32[]{:S(2)}) %collective-permute-start.6) | collective-permute-done | bytes 49184 | tf_op jit(solution)/shard_map/ppermute | solution.py:517
  117.6 1.8 %copy-done.2 = f32[5,8,48,384]{3,2,1,0:T(8,128)S(1)} copy-done((f32[5,8,48,384]{3,2,1,0:T(8,128)S(1)}, f32[5,8,48,384]{3,2,1,0:T(8,128)}, u32[]{:S(2)}) %copy-start.2) | copy-done | bytes 2949144
  119.5 0.5 zonal.1.zonal_ref
  120.0 0.7 copy-done.9
  120.7 0.7 copy-done.12
  121.4 4.7 %final.1 = f32[5,8,45,360]{3,2,1,0:T(8,128)S(1)} custom-call(s32[2]{0:T(128)S(1)} %pad_add_fusion.ids_ref, s32[128]{0:T(128)S(1)} %copy-done.12, f32[64,24,128]{2,1,0:T(8,128)} %all-to-all-done.1.in_ref, f32[4,8,48,384]{3,2,1,0:T(8,128)S(1)} %get-tuple-element.24.p2_ref.next_ref, f32[2,8,48,384]{3,2,1,0:T(8,128)S(1)} %zonal.1.zonal_ref, ...), custom_call_target="tpu_custom_call" | custom-call | flops 1000000000 | bytes 8388608 | tf_op jit(solution)/shard_map/final/pallas_call | solution.py:486
  126.1 2.4 %copy.15 = f32[5,8,45,360]{3,1,2,0:T(8,128)} copy(f32[5,8,45,360]{3,2,1,0:T(8,128)S(1)} %final.1) | data formatting | bytes 5184000 | tf_op jit(solution)/shard_map/final/pallas_call | solution.py:486
  (31 shorter events, 0.3 us)
Async XLA Ops:
  2.5 22.3 %copy-start.8 = (s32[8,512]{1,0:T(8,128)S(1)}, s32[8,512]{1,0:T(8,128)}, u32[]{:S(2)}) copy-start(s32[8,512]{1,0:T(8,128)} %constant.46.clone.slot_ref) | copy-start | bytes 49156
  2.5 22.3 %copy-start.11 = (s32[128]{0:T(128)S(1)}, s32[128]{0:T(128)}, u32[]{:S(2)}) copy-start(s32[128]{0:T(128)} %rows_ref.5) | copy-start | bytes 1540
  3.8 13.1 %collective-permute-start = (f32[4,8,384]{2,1,0:T(8,128)S(1)}, f32[4,8,384]{2,1,0:T(8,128)S(1)}, u32[]{:S(2)}, u32[]{:S(2)}) collective-permute-start(f32[4,8,384]{2,1,0:T(8,128)S(1)} %get-tuple-element.16), channel_id=1, source_target_pairs={{0,1},{1,2},{2,3},{3,4},{4,5},{5,6},{6,7},{7,8},{8,9},{9,10},{10,1... | collective-permute-start | bytes 147464 | tf_op jit(solution)/shard_map/ppermute | solution.py:517
  5.9 10.9 %collective-permute-start.1 = (f32[4,8,384]{2,1,0:T(8,128)S(1)}, f32[4,8,384]{2,1,0:T(8,128)S(1)}, u32[]{:S(2)}, u32[]{:S(2)}) collective-permute-start(f32[4,8,384]{2,1,0:T(8,128)S(1)} %get-tuple-element.17), channel_id=1, source_target_pairs={{1,0},{2,1},{3,2},{4,3},{5,4},{6,5},{7,6},{8,7},{9,8},{10,9},{11,1... | collective-permute-start | bytes 147464 | tf_op jit(solution)/shard_map/ppermute | solution.py:518
  13.8 1.7 %collective-permute-start.2 = (f32[2,1152]{1,0:T(2,128)S(1)}, f32[2,1152]{1,0:T(2,128)S(1)}, u32[]{:S(2)}, u32[]{:S(2)}) collective-permute-start(f32[2,1152]{1,0:T(2,128)S(1)} %get-tuple-element.18), channel_id=1, source_target_pairs={{0,64},{64,0},{128,192},{192,128},{1,65},{65,1},{129,193},{193,129... | collective-permute-start | bytes 27656 | tf_op jit(solution)/shard_map/ppermute | solution.py:515
  13.8 3.1 %collective-permute-start.3 = (f32[2,1152]{1,0:T(2,128)S(1)}, f32[2,1152]{1,0:T(2,128)S(1)}, u32[]{:S(2)}, u32[]{:S(2)}) collective-permute-start(f32[2,1152]{1,0:T(2,128)S(1)} %get-tuple-element.19), channel_id=1, source_target_pairs={{64,128},{128,64},{0,32},{192,224},{65,129},{129,65},{1,33},{193,2... | collective-permute-start | bytes 27656 | tf_op jit(solution)/shard_map/ppermute | solution.py:516
  19.6 46.4 %copy-start.7 = (bf16[128,144]{1,0:T(8,128)(2,1)S(1)}, bf16[128,144]{1,0:T(8,128)(2,1)}, u32[]{:S(2)}) copy-start(bf16[128,144]{1,0:T(8,128)(2,1)} %constant.51.clone.inv_ref) | copy-start | bytes 110596
  19.6 46.4 %copy-start.10 = (bf16[80,192]{1,0:T(8,128)(2,1)S(1)}, bf16[80,192]{1,0:T(8,128)(2,1)}, u32[]{:S(2)}) copy-start(bf16[80,192]{1,0:T(8,128)(2,1)} %constant.47.clone.fwd_ref) | copy-start | bytes 92164
  19.6 46.4 %copy-start.13 = (s32[128]{0:T(128)S(1)}, s32[128]{0:T(128)}, u32[]{:S(2)}) copy-start(s32[128]{0:T(128)} %cut_ref.1) | copy-start | bytes 1540
  19.7 3.7 %collective-permute-start.4 = (f32[2,1152]{1,0:T(2,128)S(1)}, f32[2,1152]{1,0:T(2,128)S(1)}, u32[]{:S(2)}, u32[]{:S(2)}) collective-permute-start(f32[2,1152]{1,0:T(2,128)S(1)} %get-tuple-element.21), channel_id=1, source_target_pairs={{0,64},{64,0},{128,192},{192,128},{1,65},{65,1},{129,193},{193,129... | collective-permute-start | bytes 27656 | tf_op jit(solution)/shard_map/ppermute | solution.py:515
  21.2 3.6 %collective-permute-start.5 = (f32[2,1152]{1,0:T(2,128)S(1)}, f32[2,1152]{1,0:T(2,128)S(1)}, u32[]{:S(2)}, u32[]{:S(2)}) collective-permute-start(f32[2,1152]{1,0:T(2,128)S(1)} %get-tuple-element.22), channel_id=1, source_target_pairs={{64,128},{128,64},{0,32},{192,224},{65,129},{129,65},{1,33},{193,2... | collective-permute-start | bytes 27656 | tf_op jit(solution)/shard_map/ppermute | solution.py:516
  29.4 1.6 %copy-start.1 = (f32[5,8,48,384]{3,2,1,0:T(8,128)}, f32[5,8,48,384]{3,2,1,0:T(8,128)S(1)}, u32[]{:S(2)}) copy-start(f32[5,8,48,384]{3,2,1,0:T(8,128)S(1)} %get-tuple-element.20.r_ref) | copy-start | bytes 8847364
  31.0 0.9 copy-start.6
  31.9 34.2 %all-to-all-start = ((f32[64,24,128]{2,1,0:T(8,128)}), f32[64,24,128]{2,1,0:T(8,128)S(1)}, u32[]{:S(2)}, u32[]{:S(2)}) async-start(f32[64,24,128]{2,1,0:T(8,128)} %copy-done.6), calls=%async_computation | async-start | bytes 1572864 | tf_op jit(solution)/shard_map/all_to_all | solution.py:570
  66.1 1.9 %copy-start = (bf16[34,192,144]{2,1,0:T(8,128)(2,1)S(1)}, bf16[34,192,144]{2,1,0:T(8,128)(2,1)}, u32[]{:S(2)}) copy-start(bf16[34,192,144]{2,1,0:T(8,128)(2,1)} %constant.48.clone.mf_ref) | copy-start | bytes 5640196
  68.0 1.4 %copy-start.3 = (bf16[17,192,192]{2,1,0:T(8,128)(2,1)S(1)}, bf16[17,192,192]{2,1,0:T(8,128)(2,1)}, u32[]{:S(2)}) copy-start(bf16[17,192,192]{2,1,0:T(8,128)(2,1)} %constant.49.clone.mi2_ref) | copy-start | bytes 3760132
  69.5 1.1 copy-start.4
  70.6 1.1 copy-start.5
  86.4 33.6 %all-to-all-start.1 = ((f32[64,24,128]{2,1,0:T(8,128)}), f32[64,24,128]{2,1,0:T(8,128)}, u32[]{:S(2)}, u32[]{:S(2)}) async-start(f32[64,24,128]{2,1,0:T(8,128)} %spectral.1), calls=%async_computation.1 | async-start | bytes 1572864 | tf_op jit(solution)/shard_map/all_to_all | solution.py:582
  92.5 25.1 %collective-permute-start.6 = (f32[4,8,384]{2,1,0:T(8,128)S(1)}, f32[4,8,384]{2,1,0:T(8,128)S(1)}, u32[]{:S(2)}, u32[]{:S(2)}) collective-permute-start(f32[4,8,384]{2,1,0:T(8,128)S(1)} %get-tuple-element.25), channel_id=1, source_target_pairs={{0,1},{1,2},{2,3},{3,4},{4,5},{5,6},{6,7},{7,8},{8,9},{9,10},{10,1... | collective-permute-start | bytes 147464 | tf_op jit(solution)/shard_map/ppermute | solution.py:517
  95.6 22.0 %collective-permute-start.7 = (f32[4,8,384]{2,1,0:T(8,128)S(1)}, f32[4,8,384]{2,1,0:T(8,128)S(1)}, u32[]{:S(2)}, u32[]{:S(2)}) collective-permute-start(f32[4,8,384]{2,1,0:T(8,128)S(1)} %get-tuple-element.26), channel_id=1, source_target_pairs={{1,0},{2,1},{3,2},{4,3},{5,4},{6,5},{7,6},{8,7},{9,8},{10,9},{11,1... | collective-permute-start | bytes 147464 | tf_op jit(solution)/shard_map/ppermute | solution.py:518
  117.6 1.8 %copy-start.2 = (f32[5,8,48,384]{3,2,1,0:T(8,128)S(1)}, f32[5,8,48,384]{3,2,1,0:T(8,128)}, u32[]{:S(2)}) copy-start(f32[5,8,48,384]{3,2,1,0:T(8,128)} %copy-done.1) | copy-start | bytes 8847364
  120.0 0.7 copy-start.9
  120.7 0.7 copy-start.12

commit v2 on v1

v2 whole, which is shorter than its diff:
```python
import jax
import jax.numpy as jnp
import ml_dtypes
import numpy as np
from jax import lax
from jax.experimental import pallas as pl
from jax.experimental.pallas import tpu as pltpu
from jax.sharding import PartitionSpec as P

NLON, NLAT, LEV = 2880, 1440, 8
SEG, BAND, FROWS, FIELDS = 45, 360, 64, 5
F32, BF16, I32 = jnp.float32, jnp.bfloat16, jnp.int32
NN = (((1,), (0,)), ((), ()))
NT = (((1,), (1,)), ((), ()))
TN = (((0,), (0,)), ((), ()))

SLOT_BASE = (0, 12, 22, 30, 38, 46, 54)
SLOT_COUNT = (12, 10, 8, 8, 8, 8, 8)
SLOT_FIRST = (-2, -1, 0, 0, 0, 0, 0)
PAIRS = 17
MROWS = 23
COLS = 2 * MROWS
EDGE = 3 * SEG * LEV


def slot_tables():
    rho = np.full(64, -100, np.int32)
    kind = np.full(64, -1, np.int32)
    for f, (base, count, first) in enumerate(zip(SLOT_BASE, SLOT_COUNT, SLOT_FIRST)):
        rho[base : base + count] = first + np.arange(count)
        kind[base : base + count] = f
    return rho, kind


def split_np(m):
    high = m.astype(ml_dtypes.bfloat16)
    low = (m - high.astype(np.float64)).astype(ml_dtypes.bfloat16)
    return high, low


def triple(m):
    high, low = split_np(m)
    return np.concatenate([high, low, high], axis=-1)


def fourier_constants():
    s = np.arange(64)
    k1 = np.arange(33)
    ang = 2 * np.pi * (np.outer(k1, s) % 64) / 64
    fwd = np.zeros((80, 64))
    fwd[:33], fwd[40:73] = np.cos(ang), -np.sin(ang)
    inv = np.zeros((2, 64, 2, 24))
    sig = np.zeros((PAIRS, 96, 128))
    mf = np.zeros((2 * PAIRS, 192, 48))
    mi = np.zeros((PAIRS, 192, 96))
    i, k2 = np.arange(SEG), np.arange(SEG)
    for q in range(33):
        half, pair = divmod(q, PAIRS)
        inv[half, :, 0, pair] = np.cos(ang[q])
        inv[half, :, 1, pair] = -np.sin(ang[q])
        k = q + 64 * k2
        w = 2 * np.pi * (np.outer(k, i) % NLON) / NLON
        full = np.zeros((2, 48, 2, 48))
        full[0, :SEG, 0, :SEG], full[0, :SEG, 1, :SEG] = np.cos(w), np.sin(w)
        full[1, :SEG, 0, :SEG], full[1, :SEG, 1, :SEG] = -np.sin(w), np.cos(w)
        for h in range(2):
            mf[q, 96 * h : 96 * h + 96] = np.stack([np.pad(full[:, :, n, h : 2 * MROWS : 2], ((0, 0), (0, 0), (0, 1))) for n in range(2)], axis=2).reshape(96, 48)
        scale = (1.0 if q in (0, 32) else 2.0) / NLON
        mi[pair, 96 * half : 96 * half + 96] = full.reshape(96, 96).T * scale
        sn = np.sin(2 * np.pi * k / NLON)
        sig[pair, :SEG, 64 * half : 64 * half + 64] = -sn[:, None]
        sig[pair, 48 : 48 + SEG, 64 * half : 64 * half + 64] = sn[:, None]
    return (
        triple(fwd),
        triple(inv.reshape(128, 48)),
        np.concatenate(split_np(mf), axis=-1),
        np.concatenate(split_np(mi), axis=-1),
        sig.astype(np.float32),
    )


def dot(a, b, dims=NN):
    return lax.dot_general(a, b, dims, preferred_element_type=F32)


def split(x):
    high = x.astype(BF16)
    return high, (x - high.astype(F32)).astype(BF16)


def iota(shape, axis):
    return lax.broadcasted_iota(I32, shape, axis)


def edge_rows(fields, even):
    r, lane = iota((16, 384), 0), iota((16, 384), 1)
    north = (r < 2) == even
    target = jnp.where(north, BAND - 1 - r % 2, r % 2)
    pick = jnp.where((lane == target) & (r < 4), 1.0, 0.0).astype(BF16)
    high, low = split(fields)
    return dot(pick, high, NT) + dot(pick, low, NT)


def placed_rows(first_ref, second_ref, rows_ref, even, polar):
    rows_ref[...] = jnp.zeros_like(rows_ref)
    rows_ref[0:2, :] = first_ref[...]
    wind = iota((2, EDGE), 1) < 720
    second = second_ref[...]
    rows_ref[2:4, :] = jnp.where(wind & polar, -second, second)
    r, lane = iota((16, 384), 0), iota((16, 384), 1)
    north = (r < 2) == even
    target = jnp.where(north, BAND + r % 2, 383 - r % 2)
    put = jnp.where((lane == target) & (r < 4), 1.0, 0.0).astype(BF16)
    high, low = split(rows_ref[...])
    return (dot(high, put, TN) + dot(low, put, TN)).reshape(3, SEG, LEV, 384)


def lat_of(ids_ref):
    b = ids_ref[0]
    return b, b % 2 == 0, (b == 0) | (b == 3)


def shift_lanes(x, by):
    return pltpu.roll(x, by % x.shape[-1], x.ndim - 1)


def level_difference(x):
    lev = iota(x.shape, x.ndim - 2)
    above = jnp.where(lev < LEV - 1, pltpu.roll(x, LEV - 1, x.ndim - 2), 0.0)
    below = jnp.where(lev > 0, pltpu.roll(x, 1, x.ndim - 2), 0.0)
    return above - below


def row_difference(x):
    return shift_lanes(x, -1) - shift_lanes(x, 1)


def edges_kernel(ids_ref, state_ref, east_ref, west_ref, first_ref, second_ref, box_ref):
    _, even, _ = lat_of(ids_ref)
    box_ref[:, :, :, 256:384] = jnp.zeros((3, SEG, LEV, 128), F32)
    for n, field in enumerate((0, 1, 3)):
        box_ref[n, :, :, 0:BAND] = state_ref[field]
    send_edges(box_ref, (0, 1, 2), even, east_ref, west_ref, first_ref, second_ref)


def send_edges(box_ref, uvp, even, east_ref, west_ref, first_ref, second_ref):
    u, v, p = uvp
    for slot, (f, col) in enumerate(((p, 43), (p, 44), (u, 44), (v, 44))):
        east_ref[slot] = box_ref[f, col]
    for slot, (f, col) in enumerate(((p, 1), (p, 0), (u, 0), (v, 0))):
        west_ref[slot] = box_ref[f, col]
    fields = jnp.concatenate([box_ref[f].reshape(360, 384) for f in uvp], axis=0)
    rows = edge_rows(fields, even)
    first_ref[...] = rows[0:2]
    second_ref[...] = rows[2:4]


def fill_columns(ext_ref, from_west_ref, from_east_ref):
    ext_ref[2, 0] = from_west_ref[0]
    ext_ref[2, 1] = from_west_ref[1]
    ext_ref[0, 1] = from_west_ref[2]
    ext_ref[1, 1] = from_west_ref[3]
    ext_ref[2, 48] = from_east_ref[0]
    ext_ref[2, 47] = from_east_ref[1]
    ext_ref[0, 47] = from_east_ref[2]
    ext_ref[1, 47] = from_east_ref[3]


CHUNKS = tuple((i, min(i + 5, SEG)) for i in range(0, SEG, 5))


def first_kernel(
    ids_ref, state_ref, from_west_ref, from_east_ref, got_first_ref, got_second_ref, tab_ref,
    out_ref, east_ref, west_ref, first_ref, second_ref, ext_ref, rows_ref, new_u_ref,
):
    _, even, polar = lat_of(ids_ref)
    ext_ref[:, 2:47] = placed_rows(got_first_ref, got_second_ref, rows_ref, even, polar)
    for n, field in enumerate((0, 1, 3)):
        ext_ref[n, 2:47, :, 0:BAND] = state_ref[field]
    fill_columns(ext_ref, from_west_ref, from_east_ref)
    a, f, c, qc = (tab_ref[n : n + 1, :] for n in range(4))
    out_ref[:, :, :, 256:384] = jnp.zeros((5, SEG, LEV, 128), F32)
    for i, end in ((-1, 0), *CHUNKS, (45, 46)):
        new_u_ref[i + 1 : end + 1] = (
            ext_ref[0, i + 2 : end + 2]
            - (0.5 * a) * (ext_ref[2, i + 3 : end + 3] - ext_ref[2, i + 1 : end + 1])
            + f * ext_ref[1, i + 2 : end + 2]
        )
    for i, end in CHUNKS:
        at = slice(i + 2, end + 2)
        p = ext_ref[2, at]
        new_v = ext_ref[1, at] - 0.25 * row_difference(p) - f * ext_ref[0, at]
        new_p = p - (0.5 * a) * (new_u_ref[i + 2 : end + 2] - new_u_ref[i:end])
        new_p -= qc * row_difference(c * new_v)
        th = state_ref[4, i:end]
        new_w = state_ref[2, i:end] - 0.25 * level_difference(state_ref[3, i:end]) + 0.3 * th
        out_ref[0, i:end, :, 0:BAND] = new_u_ref[i + 1 : end + 1, :, 0:BAND]
        out_ref[1, i:end, :, 0:BAND] = new_v[:, :, 0:BAND]
        out_ref[2, i:end, :, 0:BAND] = new_w
        out_ref[3, i:end, :, 0:BAND] = new_p[:, :, 0:BAND] - 0.25 * level_difference(new_w)
        out_ref[4, i:end, :, 0:BAND] = th - 0.3 * new_w
    send_edges(out_ref, (0, 1, 3), even, east_ref, west_ref, first_ref, second_ref)


def row_lanes(ids_ref, rows_ref, index):
    b = ids_ref[0]
    at = jnp.where(b >= 2, FROWS, 0)
    lane = jnp.full(index.shape, -1, I32)
    for k in range(FROWS):
        e = rows_ref[at + k] - BAND * b
        e = jnp.where(e < 0, jnp.where(e >= -2, e + 384, -1), jnp.where(e <= BAND + 1, e, -1))
        lane = jnp.where(index == k, e, lane)
    return lane


def pack_kernel(
    ids_ref, rows_ref, r_ref, got_first_ref, got_second_ref, tab_ref, slot_ref,
    out_ref, next_ref, x_ref, edge_ref, placed_ref,
):
    _, even, polar = lat_of(ids_ref)
    placed_ref[...] = placed_rows(got_first_ref, got_second_ref, edge_ref, even, polar)
    a, f, c, qc = (tab_ref[n : n + 1, :] for n in range(4))
    for i in range(0, SEG, 6):
        end = min(i + 6, SEG)
        at = slice(i, end)
        u = r_ref[0, at] + placed_ref[0, at]
        v = r_ref[1, at] + placed_ref[1, at]
        p = r_ref[3, at] + placed_ref[2, at]
        th = r_ref[4, at]
        g = v - f * u
        new_v = g - 0.25 * row_difference(p)
        new_w = r_ref[2, at] - 0.25 * level_difference(p) + 0.3 * th
        new_p = p - qc * row_difference(c * new_v) - 0.25 * level_difference(new_w)
        new_t = th - 0.3 * new_w
        for n, value in enumerate((new_v, new_w, new_p, new_t)):
            next_ref[n, at] = value
        rows = slice(LEV * i, LEV * (end + (end - i) % 2))
        for n, value in enumerate((p, g, u + f * v, new_v, new_w, new_p, new_t)):
            if (end - i) % 2:
                value = jnp.concatenate([value, jnp.zeros((1, LEV, 384), F32)], axis=0)
            high, low = split(value.reshape(-1, 384))
            x_ref[0, rows, 384 * n : 384 * n + 384] = high
            x_ref[1, rows, 384 * n : 384 * n + 384] = low
    lane = row_lanes(ids_ref, rows_ref, slot_ref[0:1, :])
    kind = slot_ref[1:2, :]
    row = iota((384, 512), 0)
    one_hot = jnp.concatenate(
        [jnp.where(row == jnp.where(kind == n, lane, -1), 1.0, 0.0).astype(BF16) for n in range(7)], axis=0
    )
    got = dot(x_ref[0], one_hot) + dot(x_ref[1], one_hot)
    low_half = iota((8, 128), 1) < 64
    for r in range(MROWS):
        for t in range(4):
            top = got[16 * r : 16 * r + 8, 128 * t : 128 * t + 128]
            bottom = got[16 * r + 8 : 16 * r + 16, 128 * t : 128 * t + 128]
            out_ref[:, 2 * t, r, :] = jnp.where(low_half, top, shift_lanes(bottom, 64))
            out_ref[:, 2 * t + 1, r, :] = jnp.where(low_half, shift_lanes(top, 64), bottom)


def zonal_kernel(r_ref, p2_ref, from_west_ref, from_east_ref, tab_ref, out_ref, ext_ref, new_u_ref):
    a, f = tab_ref[0:1, :], tab_ref[1:2, :]
    for n, field in enumerate((0, 1, 3)):
        ext_ref[n, 2:47] = r_ref[field]
    fill_columns(ext_ref, from_west_ref, from_east_ref)
    for i, end in ((-1, 0), *CHUNKS, (45, 46)):
        new_u_ref[i + 1 : end + 1] = (
            ext_ref[0, i + 2 : end + 2]
            - (0.5 * a) * (ext_ref[2, i + 3 : end + 3] - ext_ref[2, i + 1 : end + 1])
            + f * ext_ref[1, i + 2 : end + 2]
        )
    for i, end in CHUNKS:
        out_ref[0, i:end] = new_u_ref[i + 1 : end + 1]
        out_ref[1, i:end] = p2_ref[2, i:end] - (0.5 * a) * (new_u_ref[i + 2 : end + 2] - new_u_ref[i:end])


def spectral_kernel(
    ids_ref, rows_ref, cut_ref, cos_ref, in_ref, slot_ref, fwd_ref, inv_ref, mf_ref, mi_ref, sig_ref,
    out_ref, z_ref, s_ref, y_ref, mix_ref,
):
    b, owner = ids_ref[0], ids_ref[1]
    at = jnp.where(b >= 2, FROWS, 0)
    first = 8 * (owner % 8)
    low_half = iota((96, 128), 1) < 64

    rho = slot_ref[2:3, 0:128]
    kind = slot_ref[3:4, 0:128]

    def listed(k):
        return jnp.where((k >= 0) & (k < FROWS), rows_ref[at + jnp.clip(k, 0, FROWS - 1)], -1000)

    row_at = [listed(first + t) for t in range(-4, 12)]
    cut_at = [cut_ref[at + jnp.clip(first + t, 0, FROWS - 1)] for t in range(-4, 12)]
    blank = jnp.zeros((1, 128), F32)
    rows = [jnp.full((1, 128), -1000, I32) for _ in range(5)]
    cut, c0, cp, cm = jnp.zeros((1, 128), I32), blank + 1.0, blank, blank
    for t in range(-2, 10):
        here = rho == t
        jc = jnp.clip(row_at[t + 4], 0, NLAT - 1)
        for d in range(-2, 3):
            rows[d + 2] = jnp.where(here, row_at[t + d + 4], rows[d + 2])
        cut = jnp.where(here, cut_at[t + 4], cut)
        cm = jnp.where(here, cos_ref[jc], cm)
        c0 = jnp.where(here, cos_ref[jc + 1], c0)
        cp = jnp.where(here, cos_ref[jc + 2], cp)
    j = rows[2]

    def yes(cond):
        return jnp.where(cond, 1.0, 0.0)

    up1, dn1 = yes(rows[3] == j + 1), yes(rows[1] == j - 1)
    up2, up22 = yes(rows[3] == j + 2), yes(rows[4] == j + 2)
    dn2, dn22 = yes(rows[1] == j - 2), yes(rows[0] == j - 2)
    south, north = yes(j == 0), yes(j == NLAT - 1)
    a = 0.5 * cos_ref[1] / c0
    qc = -0.25 / c0
    src, dst = iota((128, 128), 0), iota((128, 128), 1)

    def mix(n, terms):
        total = jnp.zeros((128, 128), F32)
        for to, shift, coef in terms:
            total += jnp.where(src == dst - shift, jnp.where(kind == to, coef, 0.0), 0.0)
        high, low = split(total)
        mix_ref[128 * n : 128 * n + 128, 0:128] = high
        mix_ref[128 * n : 128 * n + 128, 128:256] = low

    q0 = -0.25 * (cp * (1 - north) + cm * (1 - south) + c0 * (south + north))
    pole = 0.25 * (north - south)
    mix(0, [(2, 20, -a), (5, 24, -a)])
    mix(1, [(5, 44, -a * a)])
    mix(
        2,
        [
            (1, 10, 0.25 * up1), (1, 12, -0.25 * dn1),
            (3, 27, 0.25 * up1), (3, 29, -0.25 * dn1), (3, 17, blank - 1.0),
            (5, 44, qc * q0),
            (5, 43, qc * 0.25 * cp * up2), (5, 42, qc * 0.25 * cp * up22),
            (5, 45, qc * 0.25 * cm * dn2), (5, 46, qc * 0.25 * cm * dn22),
            (5, 32, -qc * cp * up1), (5, 34, qc * cm * dn1),
        ],
    )
    mix(
        3,
        [
            (1, 11, pole), (3, 28, pole),
            (5, 43, qc * 0.25 * (cp * yes(j == NLAT - 2) + c0 * south * up1)),
            (5, 45, qc * 0.25 * (cm * yes(j == 1) + c0 * north * dn1)),
            (5, 33, qc * c0 * (north - south)),
        ],
    )

    z_ref[:, MROWS, :] = jnp.zeros((40, 128), F32)
    z_ref[:, 24 + MROWS, :] = jnp.zeros((40, 128), F32)
    for r in range(0, MROWS, 2):
        pieces = []
        for q in range(r, min(r + 2, MROWS)):
            high, low = split(in_ref[:, q, :])
            pieces.append(jnp.concatenate([high, high, low], axis=0))
        z = dot(fwd_ref[...], pieces[0] if len(pieces) == 1 else jnp.concatenate(pieces, axis=1))
        for n in range(len(pieces)):
            z_ref[:, r + n, :] = z[0:40, 128 * n : 128 * n + 128]
            z_ref[:, 24 + r + n, :] = z[40:80, 128 * n : 128 * n + 128]

    def both_pieces(x):
        high, low = split(x)
        return jnp.concatenate(
            [jnp.concatenate([high, low], axis=1), jnp.concatenate([high, jnp.zeros_like(low)], axis=1)], axis=0
        )

    for pair in range(PAIRS):
        parts = []
        for half in range(2):
            got = dot(mf_ref[pair + PAIRS * half], both_pieces(z_ref[pair + PAIRS * half]))
            parts.append(got[:, 0:128] + got[:, 128:256])
        s_ref[pair] = jnp.where(
            low_half,
            parts[0][0:96] + shift_lanes(parts[0][96:192], 64),
            shift_lanes(parts[1][0:96], 64) + parts[1][96:192],
        )
    final = kind >= 2
    sign = jnp.where(kind == 1, -1.0, 1.0)
    k_base = 64 * (iota((96, 128), 0) % 48) + jnp.where(low_half, 0, PAIRS)
    odd_base = jnp.where(low_half, 1.0, -1.0)
    for pair in range(PAIRS):
        s = s_ref[pair]
        k = k_base + pair
        keep = jnp.minimum(k, NLON - k) <= cut
        h = jnp.where(keep, 0.0, s)
        sig = sig_ref[pair]
        d = sig * jnp.concatenate([s[48:96], s[0:48]], axis=0)
        ph = (odd_base if pair % 2 == 0 else -odd_base) * h
        high, low = split(jnp.concatenate([d, sig * sig * s, h, ph], axis=1))
        corr = dot(high, mix_ref[...])
        corr = corr[:, 0:128] + corr[:, 128:256] + dot(low, mix_ref[:, 0:128])
        s_ref[pair] = jnp.where(final, jnp.where(keep, s + corr, 0.0), sign * h + corr)
    y_ref[PAIRS:24] = jnp.zeros((24 - PAIRS, 96, 128), F32)
    for pair in range(PAIRS):
        back = dot(mi_ref[pair], both_pieces(s_ref[pair]))
        back = back[:, 0:128] + back[:, 128:256]
        y_ref[pair] = jnp.where(low_half, back[0:96], back[96:192])
    half64 = iota((64, 128), 1) < 64
    for r in range(MROWS):
        cols = []
        for i in (2 * r, 2 * r + 1):
            zz = jnp.concatenate([y_ref[:, i, :], y_ref[:, 48 + i, :]], axis=0)
            high, low = split(zz)
            cols.append(jnp.concatenate([high, high, low], axis=0))
        x = dot(inv_ref[...], jnp.concatenate(cols, axis=1))
        out_ref[:, r, :] = jnp.where(
            half64,
            x[0:64, 0:128] + shift_lanes(x[64:128, 0:128], 64),
            shift_lanes(x[0:64, 128:256], 64) + x[64:128, 128:256],
        )


def final_kernel(ids_ref, rows_ref, in_ref, next_ref, zonal_ref, tab_ref, slot_ref, out_ref, piece_ref):
    low_half = iota((8, 128), 1) < 64
    for r in range(MROWS):
        for t in range(4):
            even, odd = in_ref[:, 2 * t, r, :], in_ref[:, 2 * t + 1, r, :]
            top = jnp.where(low_half, even, shift_lanes(odd, 64))
            bottom = jnp.where(low_half, shift_lanes(even, 64), odd)
            high, low = split(jnp.concatenate([top, bottom], axis=0))
            piece_ref[0, 16 * r : 16 * r + 16, 128 * t : 128 * t + 128] = high
            piece_ref[1, 16 * r : 16 * r + 16, 128 * t : 128 * t + 128] = low
    rho = slot_ref[2:3, :]
    own = (rho >= 0) & (rho < 8)
    lane = row_lanes(ids_ref, rows_ref, slot_ref[0:1, :])
    kind = slot_ref[1:2, :]
    row = iota((384, 512), 0)

    def spread(n):
        one_hot = jnp.where(row == jnp.where((kind == n) & own, lane, -1), 1.0, 0.0).astype(BF16)
        return (dot(piece_ref[0], one_hot, NT) + dot(piece_ref[1], one_hot, NT)).reshape(COLS, LEV, 384)

    flag = jnp.zeros((1, 384), F32)
    at = jnp.where(ids_ref[0] >= 2, FROWS, 0)
    lanes = iota((1, 384), 1)
    for k in range(FROWS):
        e = rows_ref[at + k] - BAND * ids_ref[0]
        e = jnp.where((e < 0) & (e >= -2), e + 384, e)
        flag = jnp.where(lanes == e, 1.0, flag)
    flagged = flag > 0.5
    c, qc = tab_ref[2:3, :], tab_ref[3:4, :]
    hp, dv = spread(0), spread(1)
    dv = jnp.where(flagged, dv, 0.25 * row_difference(hp))
    dp = -qc * row_difference(c * dv)

    def put(field, n, plain):
        out_ref[field] = jnp.where(flagged, spread(n)[0:SEG], plain)[:, :, 0:BAND]

    put(1, 3, next_ref[0] + dv[0:SEG])
    put(3, 5, zonal_ref[1] + dp[0:SEG])
    put(0, 2, zonal_ref[0])
    put(2, 4, next_ref[1])
    put(4, 6, next_ref[3])


VMEM = pl.BlockSpec(memory_space=pltpu.VMEM)
SMEM = pl.BlockSpec(memory_space=pltpu.SMEM)


def call(body, name, specs, args, outs, scratch, flops, mib):
    return pl.pallas_call(
        body,
        name=name,
        out_shape=outs,
        in_specs=list(specs),
        out_specs=jax.tree.map(lambda _: VMEM, outs),
        scratch_shapes=scratch,
        compiler_params=pltpu.CompilerParams(vmem_limit_bytes=mib << 20),
        cost_estimate=pl.CostEstimate(flops=flops, bytes_accessed=8 << 20, transcendentals=0),
    )(*args)


def shape(*dims):
    return jax.ShapeDtypeStruct(dims, F32)


def neighbours():
    first, second = [], []
    for l in range(64):
        for b in (0, 2):
            first += [(64 * b + l, 64 * b + 64 + l), (64 * b + 64 + l, 64 * b + l)]
        second += [(64 + l, 128 + l), (128 + l, 64 + l)]
        second += [(l, (l + 32) % 64), (192 + l, 192 + (l + 32) % 64)]
    return first, second


def exchange(edges):
    east, west, first, second = edges
    pairs_first, pairs_second = neighbours()
    got_first = lax.ppermute(first, ("lat", "lon"), pairs_first)
    got_second = lax.ppermute(second, ("lat", "lon"), pairs_second)
    from_west = lax.ppermute(east, "lon", [(i, (i + 1) % 64) for i in range(64)])
    from_east = lax.ppermute(west, "lon", [((i + 1) % 64, i) for i in range(64)])
    return from_west, from_east, got_first, got_second


def row_tables(b):
    def cosine(row):
        return jnp.abs(jnp.sin((row.astype(F32) + 0.5) * (jnp.pi / NLAT)))

    lane = jnp.arange(384, dtype=I32)
    row = jnp.where(lane < 370, lane, lane - 384) + BAND * b
    c = cosine(row)
    f = -0.2 * jnp.cos((row.astype(F32) + 0.5) * (jnp.pi / NLAT))
    polar = cosine(jnp.zeros((), I32))
    zero = jnp.zeros_like(c)
    tab = jnp.stack([0.5 * polar / c, f, c, 0.25 / c, zero, zero, zero, zero])
    return tab, cosine(jnp.arange(-1, 1447, dtype=I32))


def per_device(prognostic, filter_rows, cutoff):
    b, lon = lax.axis_index("lat"), lax.axis_index("lon")
    ids = jnp.stack([b, lon]).astype(I32)
    tab, cosines = row_tables(b)
    tab, cosines = lax.optimization_barrier((tab, cosines))
    rho64, kind64 = slot_tables()
    slots = np.full((8, 512), -1, np.int32)
    slots[0] = (8 * np.arange(8)[:, None] + rho64[None, :]).reshape(-1)
    slots[1] = np.tile(kind64, 8)
    slots[2] = np.tile(rho64, 8)
    slots[3] = np.tile(kind64, 8)
    margin = (slots[2] < 0) | (slots[2] > 7)
    slots[3] = np.where(margin & (slots[1] == 1), 0, slots[3])
    slots = jnp.asarray(slots)
    constants = [jnp.asarray(x) for x in fourier_constants()]

    start = prognostic.transpose(0, 2, 1, 3)
    edge_shapes = (shape(4, 8, 384), shape(4, 8, 384), shape(2, EDGE), shape(2, EDGE))
    edges = call(
        edges_kernel, "edges", (SMEM, VMEM), (ids, start), edge_shapes,
        [pltpu.VMEM((3, SEG, LEV, 384), F32)], 10**7, 16,
    )
    state, *edges = call(
        first_kernel, "first", (SMEM, *[VMEM] * 6), (ids, start, *exchange(edges), tab),
        (shape(5, SEG, LEV, 384), *edge_shapes),
        [pltpu.VMEM((3, 49, LEV, 384), F32), pltpu.VMEM((16, EDGE), F32), pltpu.VMEM((47, LEV, 384), F32)],
        10**8, 24,
    )
    from_west, from_east, got_first, got_second = exchange(edges)
    message, after = call(
        pack_kernel, "pack", (SMEM, SMEM, *[VMEM] * 5),
        (ids, filter_rows, state, got_first, got_second, tab, slots),
        (shape(8, 8, MROWS, 128), shape(4, SEG, LEV, 384)),
        [
            pltpu.VMEM((2, LEV * COLS, 7 * 384), BF16),
            pltpu.VMEM((16, EDGE), F32),
            pltpu.VMEM((3, SEG, LEV, 384), F32),
        ],
        10**9, 32,
    )
    zonal = call(
        zonal_kernel, "zonal", [VMEM] * 5, (state, after, from_west, from_east, tab),
        shape(2, SEG, LEV, 384),
        [pltpu.VMEM((3, 49, LEV, 384), F32), pltpu.VMEM((47, LEV, 384), F32)], 10**8, 16,
    )
    message, zonal = lax.optimization_barrier((message, zonal))
    whole = lax.all_to_all(message.reshape(64, MROWS, 128), "lon", split_axis=0, concat_axis=0, tiled=True)
    answer = call(
        spectral_kernel, "spectral", (*[SMEM] * 4, *[VMEM] * 7),
        (ids, filter_rows, cutoff, cosines, whole, slots, *constants),
        shape(64, MROWS, 128),
        [
            pltpu.VMEM((40, 48, 128), F32),
            pltpu.VMEM((PAIRS, 96, 128), F32),
            pltpu.VMEM((24, 96, 128), F32),
            pltpu.VMEM((512, 256), BF16),
        ],
        10**9, 32,
    )
    back = lax.all_to_all(answer, "lon", split_axis=0, concat_axis=0, tiled=True)
    out = call(
        final_kernel, "final", (SMEM, SMEM, *[VMEM] * 5),
        (ids, filter_rows, back.reshape(8, 8, MROWS, 128), after, zonal, tab, slots),
        shape(FIELDS, SEG, LEV, BAND),
        [pltpu.VMEM((2, LEV * COLS, 512), BF16)], 10**9, 32,
    )
    return out.transpose(0, 2, 1, 3)


def solution(mesh):
    in_specs = (P(None, None, "lon", "lat"), P(), P())
    out_specs = P(None, None, "lon", "lat")
    return jax.shard_map(
        per_device, mesh=mesh, in_specs=in_specs, out_specs=out_specs, check_vma=False
    )
```

time: 129 us -> 108 us (0.84)
  the two profiles are of different devices: /device:TPU:2 before, /device:TPU:8 now
where the time goes in v2:
time: 108 us; the launch traced here: 107 us
  blocking collectives  60.5 us (56%)
  Pallas kernels  22.2 us (21%)
  starting transfers between devices  20.2 us (19%)
  waiting for transfers between devices  2.35 us (2%)
  local copies, waits for them, and re-layouts  1.86 us (2%)
    all_to_all x1, blocking collectives, per_device(): lax.all_to_all(message.reshape(64, MROWS, 128), 'lon', split_axis=0, conc...  31.3 us
    all_to_all x1, blocking collectives, per_device(): lax.all_to_all(answer, 'lon', split_axis=0, concat_axis=0, tiled=True)  29.1 us
    pallas_call x6, Pallas kernels, call(): pl.pallas_call(body, name=name, out_shape=outs, in_specs=list(specs), out...  22.2 us
    ppermute x2, starting transfers between devices, exchange(): lax.ppermute(west, 'lon', [((i + 1) % 64, i) for i in range(64)])  11.8 us
    ppermute x2, starting transfers between devices, exchange(): got_second = lax.ppermute(second, ('lat', 'lon'), pairs_second)  5.26 us
    ppermute x2, starting transfers between devices, exchange(): lax.ppermute(east, 'lon', [(i, (i + 1) % 64) for i in range(64)])  3.08 us
    ppermute x2, waiting for transfers between devices, exchange(): got_second = lax.ppermute(second, ('lat', 'lon'), pairs_second)  2.33 us
  transfers between devices with their start and end apart: 8, of which 1 were waited for; matrix products, arithmetic and copies ran while one was open for 0% of the time, Pallas kernels for 5%

profile of v2, /device:TPU:8, one launch (start us, length us, event | category | flops | bytes accessed | tf_op | source)
XLA Modules:
  0.0 107.5 jit_solution(13364637139426955495)
XLA Ops:
  0.0 0.1 pad_add_fusion.ids_ref
  0.1 1.8 %copy-done = f32[5,8,45,360]{3,1,2,0:T(8,128)S(1)} copy-done((f32[5,8,45,360]{3,1,2,0:T(8,128)S(1)}, f32[5,8,45,360]{3,1,2,0:T(8,128)}, u32[]{:S(2)}) %copy-start) | copy-done | bytes 2592024
  1.9 1.2 %edges.1 = (f32[4,8,384]{2,1,0:T(8,128)S(1)}, f32[4,8,384]{2,1,0:T(8,128)S(1)}, f32[2,1080]{1,0:T(2,128)S(1)}, f32[2,1080]{1,0:T(2,128)S(1)}) custom-call(s32[2]{0:T(128)S(1)} %pad_add_fusion.ids_ref, f32[5,45,8,360]{3,2,1,0:T(8,128)S(1)} %bitcast.6), custom_call_target="tpu_custom_call" | custom-call | flops 10000000 | bytes 8388608 | tf_op jit(solution)/shard_map/edges/pallas_call | solution.py:463
  3.1 3.1 %collective-permute-start = (f32[4,8,384]{2,1,0:T(8,128)S(1)}, f32[4,8,384]{2,1,0:T(8,128)S(1)}, u32[]{:S(2)}, u32[]{:S(2)}) collective-permute-start(f32[4,8,384]{2,1,0:T(8,128)S(1)} %get-tuple-element.21), channel_id=1, source_target_pairs={{0,1},{1,2},{2,3},{3,4},{4,5},{5,6},{6,7},{7,8},{8,9},{9,10},{10,1... | collective-permute-start | bytes 147464 | tf_op jit(solution)/shard_map/ppermute | solution.py:494
  6.1 5.3 %collective-permute-start.1 = (f32[4,8,384]{2,1,0:T(8,128)S(1)}, f32[4,8,384]{2,1,0:T(8,128)S(1)}, u32[]{:S(2)}, u32[]{:S(2)}) collective-permute-start(f32[4,8,384]{2,1,0:T(8,128)S(1)} %get-tuple-element.22), channel_id=1, source_target_pairs={{1,0},{2,1},{3,2},{4,3},{5,4},{6,5},{7,6},{8,7},{9,8},{10,9},{11,1... | collective-permute-start | bytes 147464 | tf_op jit(solution)/shard_map/ppermute | solution.py:495
  11.4 0.0 collective-permute-start.2
  11.4 2.6 %collective-permute-start.3 = (f32[2,1080]{1,0:T(2,128)S(1)}, f32[2,1080]{1,0:T(2,128)S(1)}, u32[]{:S(2)}, u32[]{:S(2)}) collective-permute-start(f32[2,1080]{1,0:T(2,128)S(1)} %get-tuple-element.24), channel_id=1, source_target_pairs={{64,128},{128,64},{0,32},{192,224},{65,129},{129,65},{1,33},{193,2... | collective-permute-start | bytes 25928 | tf_op jit(solution)/shard_map/ppermute | solution.py:493
  14.0 0.1 sine_abs_fusion.cos_ref
  14.1 0.1 broadcast_divide_fusion
  14.1 0.1 cosine_multiply_fusion
  14.2 0.0 collective-permute-done.2.got_first_ref
  14.2 2.3 %collective-permute-done.3.got_second_ref = f32[2,1080]{1,0:T(2,128)S(1)} collective-permute-done((f32[2,1080]{1,0:T(2,128)S(1)}, f32[2,1080]{1,0:T(2,128)S(1)}, u32[]{:S(2)}, u32[]{:S(2)}) %collective-permute-start.3) | collective-permute-done | bytes 8672 | tf_op jit(solution)/shard_map/ppermute | solution.py:493
  16.6 0.0 collective-permute-done.from_west_ref
  16.6 0.0 collective-permute-done.1.from_east_ref
  16.6 2.3 %first.1 = (f32[5,45,8,384]{3,2,1,0:T(8,128)S(1)}, f32[4,8,384]{2,1,0:T(8,128)S(1)}, f32[4,8,384]{2,1,0:T(8,128)S(1)}, f32[2,1080]{1,0:T(2,128)S(1)}, f32[2,1080]{1,0:T(2,128)S(1)}) custom-call(s32[2]{0:T(128)S(1)} %pad_add_fusion.ids_ref, f32[5,45,8,360]{3,2,1,0:T(8,128)S(1)} %bitcast.7, f32[4,8,384]{2,1,0:T(8,128)S(1)} %collective-permute-done.from_west_ref, ...), custom_call_target="tpu_custom_call" | custom-call | flops 100000000 | bytes 8388608 | tf_op jit(solution)/shard_map/first/pallas_call | solution.py:463
  18.9 0.0 collective-permute-start.4
  18.9 2.7 %collective-permute-start.5 = (f32[2,1080]{1,0:T(2,128)S(1)}, f32[2,1080]{1,0:T(2,128)S(1)}, u32[]{:S(2)}, u32[]{:S(2)}) collective-permute-start(f32[2,1080]{1,0:T(2,128)S(1)} %get-tuple-element.28), channel_id=1, source_target_pairs={{64,128},{128,64},{0,32},{192,224},{65,129},{129,65},{1,33},{193,2... | collective-permute-start | bytes 25928 | tf_op jit(solution)/shard_map/ppermute | solution.py:493
  21.6 0.0 collective-permute-start.6
  21.6 6.5 %collective-permute-start.7 = (f32[4,8,384]{2,1,0:T(8,128)S(1)}, f32[4,8,384]{2,1,0:T(8,128)S(1)}, u32[]{:S(2)}, u32[]{:S(2)}) collective-permute-start(f32[4,8,384]{2,1,0:T(8,128)S(1)} %get-tuple-element.32), channel_id=1, source_target_pairs={{1,0},{2,1},{3,2},{4,3},{5,4},{6,5},{7,6},{8,7},{9,8},{10,9},{11,1... | collective-permute-start | bytes 147464 | tf_op jit(solution)/shard_map/ppermute | solution.py:495
  28.1 0.0 collective-permute-done.4.got_first_ref
  28.1 5.0 %pack.1 = (f32[8,8,23,128]{3,2,1,0:T(8,128)S(1)}, f32[4,45,8,384]{3,2,1,0:T(8,128)S(1)}) custom-call(s32[2]{0:T(128)S(1)} %pad_add_fusion.ids_ref, s32[128]{0:T(128)S(1)} %copy-done.8, f32[5,45,8,384]{3,2,1,0:T(8,128)S(1)} %get-tuple-element.26.r_ref, f32[2,1080]{1,0:T(2,128)S(1)} %collective-permute-done.4.got_first_ref, ...), custom_call_target="tpu_custom_call" | custom-call | flops 1000000000 | bytes 8388608 | tf_op jit(solution)/shard_map/pack/pallas_call | solution.py:463
  33.2 0.0 copy-start.2
  33.2 0.0 copy-start.3
  33.2 0.0 copy-start.4
  33.2 0.0 copy-start.5
  33.2 0.0 copy-start.7
  33.2 0.0 copy-start.9
  33.2 0.2 zonal.1.zonal_ref
  33.4 31.3 %all_to_all.10.in_ref = f32[64,23,128]{2,1,0:T(8,128)S(1)} all-to-all(f32[64,23,128]{2,1,0:T(8,128)S(1)} %bitcast.9), channel_id=1, replica_groups=mesh['lat'=4,'lon'=64] {'lon'}, dimensions={0} | all-to-all | bytes 1507328 | tf_op jit(solution)/shard_map/all_to_all | solution.py:559
  64.8 7.5 %spectral.1 = f32[64,23,128]{2,1,0:T(8,128)S(1)} custom-call(s32[2]{0:T(128)S(1)} %pad_add_fusion.ids_ref, s32[128]{0:T(128)S(1)} %copy-done.8, s32[128]{0:T(128)S(1)} %copy-done.9, f32[1448]{0:T(1024)S(1)} %sine_abs_fusion.cos_ref, f32[64,23,128]{2,1,0:T(8,128)S(1)} %all_to_all.10.in_ref, s32[8,512]{1,0:T(8,128)S(1)} %copy-done.6, ...), custom_call_target="tpu_custom_call" | custom-call | flops 1000000000 | bytes 8388608 | tf_op jit(solution)/shard_map/spectral/pallas_call | solution.py:463
  72.3 29.1 %all_to_all.11 = f32[64,23,128]{2,1,0:T(8,128)S(1)} all-to-all(f32[64,23,128]{2,1,0:T(8,128)S(1)} %spectral.1), channel_id=1, replica_groups=mesh['lat'=4,'lon'=64] {'lon'}, dimensions={0} | all-to-all | bytes 1507328 | tf_op jit(solution)/shard_map/all_to_all | solution.py:572
  101.4 6.1 %final.1 = f32[5,45,8,360]{3,2,1,0:T(8,128)} custom-call(s32[2]{0:T(128)S(1)} %pad_add_fusion.ids_ref, s32[128]{0:T(128)S(1)} %copy-done.8, f32[8,8,23,128]{3,2,1,0:T(8,128)S(1)} %bitcast.8, f32[4,45,8,384]{3,2,1,0:T(8,128)S(1)} %get-tuple-element.30.p2_ref.next_ref, f32[2,45,8,384]{3,2,1,0:T(8,128)S(1)} %zonal.1.zonal_ref, f32[8,384]{1,0:T(8,128)S(1)} %stack.23.tab_ref, ...), custom_call_target="tpu_custom_call" | custom-call | flops 1000000000 | bytes 8388608 | tf_op jit(solution)/shard_map/final/pallas_call | solution.py:463
  (18 shorter events, 0.1 us)
Async XLA Ops:
  0.1 1.8 %copy-start = (f32[5,8,45,360]{3,1,2,0:T(8,128)S(1)}, f32[5,8,45,360]{3,1,2,0:T(8,128)}, u32[]{:S(2)}) copy-start(f32[5,8,45,360]{3,1,2,0:T(8,128)} %param.9) | copy-start | bytes 7776004
  1.9 14.7 %copy-start.1 = (f32[5,8,45,360]{3,1,2,0:T(8,128)S(1)}, f32[5,8,45,360]{3,1,2,0:T(8,128)}, u32[]{:S(2)}) copy-start(f32[5,8,45,360]{3,1,2,0:T(8,128)} %param.9) | copy-start | bytes 7776004
  1.9 26.3 %copy-start.6 = (s32[8,512]{1,0:T(8,128)S(1)}, s32[8,512]{1,0:T(8,128)}, u32[]{:S(2)}) copy-start(s32[8,512]{1,0:T(8,128)} %constant.44.clone.slot_ref) | copy-start | bytes 49156
  1.9 26.3 %copy-start.8 = (s32[128]{0:T(128)S(1)}, s32[128]{0:T(128)}, u32[]{:S(2)}) copy-start(s32[128]{0:T(128)} %rows_ref.5) | copy-start | bytes 1540
  3.1 13.5 %collective-permute-start = (f32[4,8,384]{2,1,0:T(8,128)S(1)}, f32[4,8,384]{2,1,0:T(8,128)S(1)}, u32[]{:S(2)}, u32[]{:S(2)}) collective-permute-start(f32[4,8,384]{2,1,0:T(8,128)S(1)} %get-tuple-element.21), channel_id=1, source_target_pairs={{0,1},{1,2},{2,3},{3,4},{4,5},{5,6},{6,7},{7,8},{8,9},{9,10},{10,1... | collective-permute-start | bytes 147464 | tf_op jit(solution)/shard_map/ppermute | solution.py:494
  6.1 10.4 %collective-permute-start.1 = (f32[4,8,384]{2,1,0:T(8,128)S(1)}, f32[4,8,384]{2,1,0:T(8,128)S(1)}, u32[]{:S(2)}, u32[]{:S(2)}) collective-permute-start(f32[4,8,384]{2,1,0:T(8,128)S(1)} %get-tuple-element.22), channel_id=1, source_target_pairs={{1,0},{2,1},{3,2},{4,3},{5,4},{6,5},{7,6},{8,7},{9,8},{10,9},{11,1... | collective-permute-start | bytes 147464 | tf_op jit(solution)/shard_map/ppermute | solution.py:495
  11.4 2.8 %collective-permute-start.2 = (f32[2,1080]{1,0:T(2,128)S(1)}, f32[2,1080]{1,0:T(2,128)S(1)}, u32[]{:S(2)}, u32[]{:S(2)}) collective-permute-start(f32[2,1080]{1,0:T(2,128)S(1)} %get-tuple-element.23), channel_id=1, source_target_pairs={{0,64},{64,0},{128,192},{192,128},{1,65},{65,1},{129,193},{193,129... | collective-permute-start | bytes 25928 | tf_op jit(solution)/shard_map/ppermute | solution.py:492
  11.4 5.2 %collective-permute-start.3 = (f32[2,1080]{1,0:T(2,128)S(1)}, f32[2,1080]{1,0:T(2,128)S(1)}, u32[]{:S(2)}, u32[]{:S(2)}) collective-permute-start(f32[2,1080]{1,0:T(2,128)S(1)} %get-tuple-element.24), channel_id=1, source_target_pairs={{64,128},{128,64},{0,32},{192,224},{65,129},{129,65},{1,33},{193,2... | collective-permute-start | bytes 25928 | tf_op jit(solution)/shard_map/ppermute | solution.py:493
  18.9 9.2 %collective-permute-start.4 = (f32[2,1080]{1,0:T(2,128)S(1)}, f32[2,1080]{1,0:T(2,128)S(1)}, u32[]{:S(2)}, u32[]{:S(2)}) collective-permute-start(f32[2,1080]{1,0:T(2,128)S(1)} %get-tuple-element.27), channel_id=1, source_target_pairs={{0,64},{64,0},{128,192},{192,128},{1,65},{65,1},{129,193},{193,129... | collective-permute-start | bytes 25928 | tf_op jit(solution)/shard_map/ppermute | solution.py:492
  18.9 9.2 %collective-permute-start.5 = (f32[2,1080]{1,0:T(2,128)S(1)}, f32[2,1080]{1,0:T(2,128)S(1)}, u32[]{:S(2)}, u32[]{:S(2)}) collective-permute-start(f32[2,1080]{1,0:T(2,128)S(1)} %get-tuple-element.28), channel_id=1, source_target_pairs={{64,128},{128,64},{0,32},{192,224},{65,129},{129,65},{1,33},{193,2... | collective-permute-start | bytes 25928 | tf_op jit(solution)/shard_map/ppermute | solution.py:493
  21.6 11.6 %collective-permute-start.6 = (f32[4,8,384]{2,1,0:T(8,128)S(1)}, f32[4,8,384]{2,1,0:T(8,128)S(1)}, u32[]{:S(2)}, u32[]{:S(2)}) collective-permute-start(f32[4,8,384]{2,1,0:T(8,128)S(1)} %get-tuple-element.31), channel_id=1, source_target_pairs={{0,1},{1,2},{2,3},{3,4},{4,5},{5,6},{6,7},{7,8},{8,9},{9,10},{10,1... | collective-permute-start | bytes 147464 | tf_op jit(solution)/shard_map/ppermute | solution.py:494
  21.6 11.6 %collective-permute-start.7 = (f32[4,8,384]{2,1,0:T(8,128)S(1)}, f32[4,8,384]{2,1,0:T(8,128)S(1)}, u32[]{:S(2)}, u32[]{:S(2)}) collective-permute-start(f32[4,8,384]{2,1,0:T(8,128)S(1)} %get-tuple-element.32), channel_id=1, source_target_pairs={{1,0},{2,1},{3,2},{4,3},{5,4},{6,5},{7,6},{8,7},{9,8},{10,9},{11,1... | collective-permute-start | bytes 147464 | tf_op jit(solution)/shard_map/ppermute | solution.py:495
  33.2 31.6 %copy-start.2 = (bf16[34,192,96]{2,1,0:T(8,128)(2,1)S(1)}, bf16[34,192,96]{2,1,0:T(8,128)(2,1)}, u32[]{:S(2)}) copy-start(bf16[34,192,96]{2,1,0:T(8,128)(2,1)} %constant.47.clone.mf_ref) | copy-start | bytes 3760132
  33.2 31.6 %copy-start.3 = (bf16[17,192,192]{2,1,0:T(8,128)(2,1)S(1)}, bf16[17,192,192]{2,1,0:T(8,128)(2,1)}, u32[]{:S(2)}) copy-start(bf16[17,192,192]{2,1,0:T(8,128)(2,1)} %constant.48.clone.mi_ref) | copy-start | bytes 3760132
  33.2 31.6 %copy-start.4 = (f32[17,96,128]{2,1,0:T(8,128)S(1)}, f32[17,96,128]{2,1,0:T(8,128)}, u32[]{:S(2)}) copy-start(f32[17,96,128]{2,1,0:T(8,128)} %constant.49.clone.sig_ref) | copy-start | bytes 2506756
  33.2 31.6 %copy-start.5 = (bf16[128,144]{1,0:T(8,128)(2,1)S(1)}, bf16[128,144]{1,0:T(8,128)(2,1)}, u32[]{:S(2)}) copy-start(bf16[128,144]{1,0:T(8,128)(2,1)} %constant.46.clone.inv_ref) | copy-start | bytes 110596
  33.2 31.6 %copy-start.7 = (bf16[80,192]{1,0:T(8,128)(2,1)S(1)}, bf16[80,192]{1,0:T(8,128)(2,1)}, u32[]{:S(2)}) copy-start(bf16[80,192]{1,0:T(8,128)(2,1)} %constant.45.clone.fwd_ref) | copy-start | bytes 92164
  33.2 31.6 %copy-start.9 = (s32[128]{0:T(128)S(1)}, s32[128]{0:T(128)}, u32[]{:S(2)}) copy-start(s32[128]{0:T(128)} %cut_ref.1) | copy-start | bytes 1540

commit v3 on v2

--- a/solution.py
+++ b/solution.py
@@ -145,10 +145,9 @@
 
 def send_edges(box_ref, uvp, even, east_ref, west_ref, first_ref, second_ref):
     u, v, p = uvp
-    for slot, (f, col) in enumerate(((p, 43), (p, 44), (u, 44), (v, 44))):
-        east_ref[slot] = box_ref[f, col]
-    for slot, (f, col) in enumerate(((p, 1), (p, 0), (u, 0), (v, 0))):
-        west_ref[slot] = box_ref[f, col]
+    for slot, (f, e, w) in enumerate(((p, 43, 1), (p, 44, 0), (u, 44, 0), (v, 44, 0))):
+        east_ref[slot] = box_ref[f, e]
+        west_ref[slot] = box_ref[f, w]
     fields = jnp.concatenate([box_ref[f].reshape(360, 384) for f in uvp], axis=0)
     rows = edge_rows(fields, even)
     first_ref[...] = rows[0:2]
@@ -156,14 +155,9 @@
 
 
 def fill_columns(ext_ref, from_west_ref, from_east_ref):
-    ext_ref[2, 0] = from_west_ref[0]
-    ext_ref[2, 1] = from_west_ref[1]
-    ext_ref[0, 1] = from_west_ref[2]
-    ext_ref[1, 1] = from_west_ref[3]
-    ext_ref[2, 48] = from_east_ref[0]
-    ext_ref[2, 47] = from_east_ref[1]
-    ext_ref[0, 47] = from_east_ref[2]
-    ext_ref[1, 47] = from_east_ref[3]
+    for slot, (f, west, east) in enumerate(((2, 0, 48), (2, 1, 47), (0, 1, 47), (1, 1, 47))):
+        ext_ref[f, west] = from_west_ref[slot]
+        ext_ref[f, east] = from_east_ref[slot]
 
 
 CHUNKS = tuple((i, min(i + 5, SEG)) for i in range(0, SEG, 5))
@@ -215,7 +209,7 @@
 
 def pack_kernel(
     ids_ref, rows_ref, r_ref, got_first_ref, got_second_ref, tab_ref, slot_ref,
-    out_ref, next_ref, x_ref, edge_ref, placed_ref,
+    out_ref, next_ref, hot_ref, x_ref, edge_ref, placed_ref,
 ):
     _, even, polar = lat_of(ids_ref)
     placed_ref[...] = placed_rows(got_first_ref, got_second_ref, edge_ref, even, polar)
@@ -244,10 +238,9 @@
     lane = row_lanes(ids_ref, rows_ref, slot_ref[0:1, :])
     kind = slot_ref[1:2, :]
     row = iota((384, 512), 0)
-    one_hot = jnp.concatenate(
-        [jnp.where(row == jnp.where(kind == n, lane, -1), 1.0, 0.0).astype(BF16) for n in range(7)], axis=0
-    )
-    got = dot(x_ref[0], one_hot) + dot(x_ref[1], one_hot)
+    for n in range(7):
+        hot_ref[384 * n : 384 * n + 384] = jnp.where(row == jnp.where(kind == n, lane, -1), 1.0, 0.0).astype(BF16)
+    got = dot(x_ref[0], hot_ref[...]) + dot(x_ref[1], hot_ref[...])
     low_half = iota((8, 128), 1) < 64
     for r in range(MROWS):
         for t in range(4):
@@ -412,7 +405,7 @@
         )
 
 
-def final_kernel(ids_ref, rows_ref, in_ref, next_ref, zonal_ref, tab_ref, slot_ref, out_ref, piece_ref):
+def final_kernel(ids_ref, rows_ref, in_ref, next_ref, zonal_ref, tab_ref, slot_ref, hot_ref, out_ref, piece_ref, done_ref, sems):
     low_half = iota((8, 128), 1) < 64
     for r in range(MROWS):
         for t in range(4):
@@ -423,13 +416,12 @@
             piece_ref[0, 16 * r : 16 * r + 16, 128 * t : 128 * t + 128] = high
             piece_ref[1, 16 * r : 16 * r + 16, 128 * t : 128 * t + 128] = low
     rho = slot_ref[2:3, :]
-    own = (rho >= 0) & (rho < 8)
-    lane = row_lanes(ids_ref, rows_ref, slot_ref[0:1, :])
-    kind = slot_ref[1:2, :]
-    row = iota((384, 512), 0)
+    own = jnp.where((rho >= 0) & (rho < 8), 1.0, 0.0).astype(BF16)
 
     def spread(n):
-        one_hot = jnp.where(row == jnp.where((kind == n) & own, lane, -1), 1.0, 0.0).astype(BF16)
+        one_hot = hot_ref[384 * n : 384 * n + 384]
+        if n < 2:
+            one_hot = one_hot * own
         return (dot(piece_ref[0], one_hot, NT) + dot(piece_ref[1], one_hot, NT)).reshape(COLS, LEV, 384)
 
     flag = jnp.zeros((1, 384), F32)
@@ -445,27 +437,34 @@
     dv = jnp.where(flagged, dv, 0.25 * row_difference(hp))
     dp = -qc * row_difference(c * dv)
 
+    stores = []
+
     def put(field, n, plain):
-        out_ref[field] = jnp.where(flagged, spread(n)[0:SEG], plain)[:, :, 0:BAND]
+        done_ref[field] = jnp.where(flagged, spread(n)[0:SEG], plain)[:, :, 0:BAND]
+        stores.append(pltpu.make_async_copy(done_ref.at[field], out_ref.at[field], sems.at[field]))
+        stores[-1].start()
 
     put(1, 3, next_ref[0] + dv[0:SEG])
     put(3, 5, zonal_ref[1] + dp[0:SEG])
     put(0, 2, zonal_ref[0])
     put(2, 4, next_ref[1])
     put(4, 6, next_ref[3])
+    for store in stores:
+        store.wait()
 
 
 VMEM = pl.BlockSpec(memory_space=pltpu.VMEM)
 SMEM = pl.BlockSpec(memory_space=pltpu.SMEM)
-
-
-def call(body, name, specs, args, outs, scratch, flops, mib):
+ANY = pl.BlockSpec(memory_space=pl.ANY)
+
+
+def call(body, name, specs, args, outs, scratch, flops, mib, out_spec=None):
     return pl.pallas_call(
         body,
         name=name,
         out_shape=outs,
         in_specs=list(specs),
-        out_specs=jax.tree.map(lambda _: VMEM, outs),
+        out_specs=jax.tree.map(lambda _: out_spec or VMEM, outs),
         scratch_shapes=scratch,
         compiler_params=pltpu.CompilerParams(vmem_limit_bytes=mib << 20),
         cost_estimate=pl.CostEstimate(flops=flops, bytes_accessed=8 << 20, transcendentals=0),
@@ -539,10 +538,10 @@
         10**8, 24,
     )
     from_west, from_east, got_first, got_second = exchange(edges)
-    message, after = call(
+    message, after, hot = call(
         pack_kernel, "pack", (SMEM, SMEM, *[VMEM] * 5),
         (ids, filter_rows, state, got_first, got_second, tab, slots),
-        (shape(8, 8, MROWS, 128), shape(4, SEG, LEV, 384)),
+        (shape(8, 8, MROWS, 128), shape(4, SEG, LEV, 384), jax.ShapeDtypeStruct((7 * 384, 512), BF16)),
         [
             pltpu.VMEM((2, LEV * COLS, 7 * 384), BF16),
             pltpu.VMEM((16, EDGE), F32),
@@ -571,10 +570,15 @@
     )
     back = lax.all_to_all(answer, "lon", split_axis=0, concat_axis=0, tiled=True)
     out = call(
-        final_kernel, "final", (SMEM, SMEM, *[VMEM] * 5),
-        (ids, filter_rows, back.reshape(8, 8, MROWS, 128), after, zonal, tab, slots),
+        final_kernel, "final", (SMEM, SMEM, *[VMEM] * 6),
+        (ids, filter_rows, back.reshape(8, 8, MROWS, 128), after, zonal, tab, slots, hot),
         shape(FIELDS, SEG, LEV, BAND),
-        [pltpu.VMEM((2, LEV * COLS, 512), BF16)], 10**9, 32,
+        [
+            pltpu.VMEM((2, LEV * COLS, 512), BF16),
+            pltpu.VMEM((FIELDS, SEG, LEV, BAND), F32),
+            pltpu.SemaphoreType.DMA((FIELDS,)),
+        ],
+        10**9, 32, ANY,
     )
     return out.transpose(0, 2, 1, 3)
 

time: 108 us -> 106 us (0.981)
  Pallas kernels: 22.2 us -> 20.9 us
  starting transfers between devices: 20.2 us -> 19.1 us
    ppermute x2, starting transfers between devices: 5.26 us -> 2.47 us  [exchange(): got_second = lax.ppermute(second, ('lat', 'lon'), pairs_second)]
    ppermute x2, waiting for transfers between devices: 2.33 us -> 0.01 us  [exchange(): got_second = lax.ppermute(second, ('lat', 'lon'), pairs_second)]
    ppermute x2, waiting for transfers between devices: 0.01 us -> 1.8 us  [exchange(): lax.ppermute(east, 'lon', [(i, (i + 1) % 64) for i in range(64)])]
    ppermute x2, starting transfers between devices: 3.08 us -> 4.47 us  [exchange(): lax.ppermute(east, 'lon', [(i, (i + 1) % 64) for i in range(64)])]
    pallas_call x6, Pallas kernels: 22.2 us -> 20.9 us  [call(): pl.pallas_call(body, name=name, out_shape=outs, in_specs=list(specs), out...]
where the time goes in v3:
time: 106 us; the launch traced here: 105 us
  blocking collectives  60.4 us (57%)
  Pallas kernels  20.9 us (20%)
  starting transfers between devices  19.1 us (18%)
  local copies, waits for them, and re-layouts  1.86 us (2%)
  waiting for transfers between devices  1.82 us (2%)
    all_to_all x1, blocking collectives, per_device(): lax.all_to_all(message.reshape(64, MROWS, 128), 'lon', split_axis=0, conc...  32 us
    all_to_all x1, blocking collectives, per_device(): lax.all_to_all(answer, 'lon', split_axis=0, concat_axis=0, tiled=True)  28.4 us
    pallas_call x6, Pallas kernels, call(): pl.pallas_call(body, name=name, out_shape=outs, in_specs=list(specs), out...  20.9 us
    ppermute x2, starting transfers between devices, exchange(): lax.ppermute(west, 'lon', [((i + 1) % 64, i) for i in range(64)])  12.1 us
    ppermute x2, starting transfers between devices, exchange(): lax.ppermute(east, 'lon', [(i, (i + 1) % 64) for i in range(64)])  4.47 us
    ppermute x2, starting transfers between devices, exchange(): got_second = lax.ppermute(second, ('lat', 'lon'), pairs_second)  2.47 us
  transfers between devices with their start and end apart: 8, of which 1 were waited for; matrix products, arithmetic and copies ran while one was open for 0% of the time, Pallas kernels for 5%

profile of v3, /device:TPU:8, one launch (start us, length us, event | category | flops | bytes accessed | tf_op | source)
XLA Modules:
  0.0 104.7 jit_solution(11466374208804796454)
XLA Ops:
  0.0 0.1 pad_add_fusion.ids_ref
  0.1 1.8 %copy-done = f32[5,8,45,360]{3,1,2,0:T(8,128)S(1)} copy-done((f32[5,8,45,360]{3,1,2,0:T(8,128)S(1)}, f32[5,8,45,360]{3,1,2,0:T(8,128)}, u32[]{:S(2)}) %copy-start) | copy-done | bytes 2592024
  1.9 1.2 %edges.1 = (f32[4,8,384]{2,1,0:T(8,128)S(1)}, f32[4,8,384]{2,1,0:T(8,128)S(1)}, f32[2,1080]{1,0:T(2,128)S(1)}, f32[2,1080]{1,0:T(2,128)S(1)}) custom-call(s32[2]{0:T(128)S(1)} %pad_add_fusion.ids_ref, f32[5,45,8,360]{3,2,1,0:T(8,128)S(1)} %bitcast.6), custom_call_target="tpu_custom_call" | custom-call | flops 10000000 | bytes 8388608 | tf_op jit(solution)/shard_map/edges/pallas_call | solution.py:462
  3.1 0.1 collective-permute-start.2
  3.1 2.4 %collective-permute-start.3 = (f32[2,1080]{1,0:T(2,128)S(1)}, f32[2,1080]{1,0:T(2,128)S(1)}, u32[]{:S(2)}, u32[]{:S(2)}) collective-permute-start(f32[2,1080]{1,0:T(2,128)S(1)} %get-tuple-element.25), channel_id=1, source_target_pairs={{64,128},{128,64},{0,32},{192,224},{65,129},{129,65},{1,33},{193,2... | collective-permute-start | bytes 25928 | tf_op jit(solution)/shard_map/ppermute | solution.py:492
  5.5 3.0 %collective-permute-start = (f32[4,8,384]{2,1,0:T(8,128)S(1)}, f32[4,8,384]{2,1,0:T(8,128)S(1)}, u32[]{:S(2)}, u32[]{:S(2)}) collective-permute-start(f32[4,8,384]{2,1,0:T(8,128)S(1)} %get-tuple-element.22), channel_id=1, source_target_pairs={{0,1},{1,2},{2,3},{3,4},{4,5},{5,6},{6,7},{7,8},{8,9},{9,10},{10,1... | collective-permute-start | bytes 147464 | tf_op jit(solution)/shard_map/ppermute | solution.py:493
  8.5 6.1 %collective-permute-start.1 = (f32[4,8,384]{2,1,0:T(8,128)S(1)}, f32[4,8,384]{2,1,0:T(8,128)S(1)}, u32[]{:S(2)}, u32[]{:S(2)}) collective-permute-start(f32[4,8,384]{2,1,0:T(8,128)S(1)} %get-tuple-element.23), channel_id=1, source_target_pairs={{1,0},{2,1},{3,2},{4,3},{5,4},{6,5},{7,6},{8,7},{9,8},{10,9},{11,1... | collective-permute-start | bytes 147464 | tf_op jit(solution)/shard_map/ppermute | solution.py:494
  14.6 0.1 sine_abs_fusion.cos_ref
  14.7 0.1 cosine_multiply_fusion
  14.8 0.1 broadcast_divide_fusion
  14.9 0.0 collective-permute-done.2.got_first_ref
  14.9 0.0 collective-permute-done.3.got_second_ref
  14.9 1.8 %collective-permute-done.from_west_ref = f32[4,8,384]{2,1,0:T(8,128)S(1)} collective-permute-done((f32[4,8,384]{2,1,0:T(8,128)S(1)}, f32[4,8,384]{2,1,0:T(8,128)S(1)}, u32[]{:S(2)}, u32[]{:S(2)}) %collective-permute-start) | collective-permute-done | bytes 49184 | tf_op jit(solution)/shard_map/ppermute | solution.py:493
  16.7 2.3 %first.1 = (f32[5,45,8,384]{3,2,1,0:T(8,128)S(1)}, f32[4,8,384]{2,1,0:T(8,128)S(1)}, f32[4,8,384]{2,1,0:T(8,128)S(1)}, f32[2,1080]{1,0:T(2,128)S(1)}, f32[2,1080]{1,0:T(2,128)S(1)}) custom-call(s32[2]{0:T(128)S(1)} %pad_add_fusion.ids_ref, f32[5,45,8,360]{3,2,1,0:T(8,128)S(1)} %bitcast.7, f32[4,8,384]{2,1,0:T(8,128)S(1)} %collective-permute-done.from_west_ref, ...), custom_call_target="tpu_custom_call" | custom-call | flops 100000000 | bytes 8388608 | tf_op jit(solution)/shard_map/first/pallas_call | solution.py:462
  19.0 0.0 collective-permute-start.4
  19.0 0.1 collective-permute-start.5
  19.1 1.4 %collective-permute-start.6 = (f32[4,8,384]{2,1,0:T(8,128)S(1)}, f32[4,8,384]{2,1,0:T(8,128)S(1)}, u32[]{:S(2)}, u32[]{:S(2)}) collective-permute-start(f32[4,8,384]{2,1,0:T(8,128)S(1)} %get-tuple-element.32), channel_id=1, source_target_pairs={{0,1},{1,2},{2,3},{3,4},{4,5},{5,6},{6,7},{7,8},{8,9},{9,10},{10,1... | collective-permute-start | bytes 147464 | tf_op jit(solution)/shard_map/ppermute | solution.py:493
  20.6 6.0 %collective-permute-start.7 = (f32[4,8,384]{2,1,0:T(8,128)S(1)}, f32[4,8,384]{2,1,0:T(8,128)S(1)}, u32[]{:S(2)}, u32[]{:S(2)}) collective-permute-start(f32[4,8,384]{2,1,0:T(8,128)S(1)} %get-tuple-element.33), channel_id=1, source_target_pairs={{1,0},{2,1},{3,2},{4,3},{5,4},{6,5},{7,6},{8,7},{9,8},{10,9},{11,1... | collective-permute-start | bytes 147464 | tf_op jit(solution)/shard_map/ppermute | solution.py:494
  26.5 0.0 collective-permute-done.4.got_first_ref
  26.5 4.8 %pack.1 = (f32[8,8,23,128]{3,2,1,0:T(8,128)S(1)}, f32[4,45,8,384]{3,2,1,0:T(8,128)S(1)}, bf16[2688,512]{1,0:T(8,128)(2,1)S(1)}) custom-call(s32[2]{0:T(128)S(1)} %pad_add_fusion.ids_ref, s32[128]{0:T(128)S(1)} %copy-done.8, f32[5,45,8,384]{3,2,1,0:T(8,128)S(1)} %get-tuple-element.27.r_ref, f32[2,1080]{1,0:T(2,128)S(1)} %collective-permute-done.4.got_first_ref, ...), custom_call_target="tpu_custom_call" | custom-call | flops 1000000000 | bytes 8388608 | tf_op jit(solution)/shard_map/pack/pallas_call | solution.py:462
  31.4 0.0 collective-permute-done.6.from_west_ref
  31.4 0.0 copy-start.2
  31.4 0.0 copy-start.3
  31.4 0.0 copy-start.4
  31.4 0.0 copy-start.5
  31.5 0.0 copy-start.7
  31.5 0.0 copy-start.9
  31.5 0.2 zonal.1.zonal_ref
  31.7 32.0 %all_to_all.10.in_ref = f32[64,23,128]{2,1,0:T(8,128)S(1)} all-to-all(f32[64,23,128]{2,1,0:T(8,128)S(1)} %bitcast.9), channel_id=1, replica_groups=mesh['lat'=4,'lon'=64] {'lon'}, dimensions={0} | all-to-all | bytes 1507328 | tf_op jit(solution)/shard_map/all_to_all | solution.py:558
  63.7 7.5 %spectral.1 = f32[64,23,128]{2,1,0:T(8,128)S(1)} custom-call(s32[2]{0:T(128)S(1)} %pad_add_fusion.ids_ref, s32[128]{0:T(128)S(1)} %copy-done.8, s32[128]{0:T(128)S(1)} %copy-done.9, f32[1448]{0:T(1024)S(1)} %sine_abs_fusion.cos_ref, f32[64,23,128]{2,1,0:T(8,128)S(1)} %all_to_all.10.in_ref, s32[8,512]{1,0:T(8,128)S(1)} %copy-done.6, ...), custom_call_target="tpu_custom_call" | custom-call | flops 1000000000 | bytes 8388608 | tf_op jit(solution)/shard_map/spectral/pallas_call | solution.py:462
  71.2 28.4 %all_to_all.11 = f32[64,23,128]{2,1,0:T(8,128)S(1)} all-to-all(f32[64,23,128]{2,1,0:T(8,128)S(1)} %spectral.1), channel_id=1, replica_groups=mesh['lat'=4,'lon'=64] {'lon'}, dimensions={0} | all-to-all | bytes 1507328 | tf_op jit(solution)/shard_map/all_to_all | solution.py:571
  99.6 4.9 %final.1 = f32[5,45,8,360]{3,2,1,0:T(8,128)} custom-call(s32[2]{0:T(128)S(1)} %pad_add_fusion.ids_ref, s32[128]{0:T(128)S(1)} %copy-done.8, f32[8,8,23,128]{3,2,1,0:T(8,128)S(1)} %bitcast.8, f32[4,45,8,384]{3,2,1,0:T(8,128)S(1)} %get-tuple-element.31.p2_ref.next_ref, f32[2,45,8,384]{3,2,1,0:T(8,128)S(1)} %zonal.1.zonal_ref, f32[8,384]{1,0:T(8,128)S(1)} %stack.23.tab_ref, ...), custom_call_target="tpu_custom_call" | custom-call | flops 1000000000 | bytes 8388608 | tf_op jit(solution)/shard_map/final/pallas_call | solution.py:462
  (18 shorter events, 0.1 us)
Async XLA Ops:
  0.1 1.8 %copy-start = (f32[5,8,45,360]{3,1,2,0:T(8,128)S(1)}, f32[5,8,45,360]{3,1,2,0:T(8,128)}, u32[]{:S(2)}) copy-start(f32[5,8,45,360]{3,1,2,0:T(8,128)} %param.9) | copy-start | bytes 7776004
  1.9 14.8 %copy-start.1 = (f32[5,8,45,360]{3,1,2,0:T(8,128)S(1)}, f32[5,8,45,360]{3,1,2,0:T(8,128)}, u32[]{:S(2)}) copy-start(f32[5,8,45,360]{3,1,2,0:T(8,128)} %param.9) | copy-start | bytes 7776004
  1.9 24.7 %copy-start.6 = (s32[8,512]{1,0:T(8,128)S(1)}, s32[8,512]{1,0:T(8,128)}, u32[]{:S(2)}) copy-start(s32[8,512]{1,0:T(8,128)} %constant.44.clone.slot_ref) | copy-start | bytes 49156
  1.9 24.7 %copy-start.8 = (s32[128]{0:T(128)S(1)}, s32[128]{0:T(128)}, u32[]{:S(2)}) copy-start(s32[128]{0:T(128)} %rows_ref.5) | copy-start | bytes 1540
  3.1 11.8 %collective-permute-start.2 = (f32[2,1080]{1,0:T(2,128)S(1)}, f32[2,1080]{1,0:T(2,128)S(1)}, u32[]{:S(2)}, u32[]{:S(2)}) collective-permute-start(f32[2,1080]{1,0:T(2,128)S(1)} %get-tuple-element.24), channel_id=1, source_target_pairs={{0,64},{64,0},{128,192},{192,128},{1,65},{65,1},{129,193},{193,129... | collective-permute-start | bytes 25928 | tf_op jit(solution)/shard_map/ppermute | solution.py:491
  3.1 11.7 %collective-permute-start.3 = (f32[2,1080]{1,0:T(2,128)S(1)}, f32[2,1080]{1,0:T(2,128)S(1)}, u32[]{:S(2)}, u32[]{:S(2)}) collective-permute-start(f32[2,1080]{1,0:T(2,128)S(1)} %get-tuple-element.25), channel_id=1, source_target_pairs={{64,128},{128,64},{0,32},{192,224},{65,129},{129,65},{1,33},{193,2... | collective-permute-start | bytes 25928 | tf_op jit(solution)/shard_map/ppermute | solution.py:492
  5.5 11.2 %collective-permute-start = (f32[4,8,384]{2,1,0:T(8,128)S(1)}, f32[4,8,384]{2,1,0:T(8,128)S(1)}, u32[]{:S(2)}, u32[]{:S(2)}) collective-permute-start(f32[4,8,384]{2,1,0:T(8,128)S(1)} %get-tuple-element.22), channel_id=1, source_target_pairs={{0,1},{1,2},{2,3},{3,4},{4,5},{5,6},{6,7},{7,8},{8,9},{9,10},{10,1... | collective-permute-start | bytes 147464 | tf_op jit(solution)/shard_map/ppermute | solution.py:493
  8.5 8.1 %collective-permute-start.1 = (f32[4,8,384]{2,1,0:T(8,128)S(1)}, f32[4,8,384]{2,1,0:T(8,128)S(1)}, u32[]{:S(2)}, u32[]{:S(2)}) collective-permute-start(f32[4,8,384]{2,1,0:T(8,128)S(1)} %get-tuple-element.23), channel_id=1, source_target_pairs={{1,0},{2,1},{3,2},{4,3},{5,4},{6,5},{7,6},{8,7},{9,8},{10,9},{11,1... | collective-permute-start | bytes 147464 | tf_op jit(solution)/shard_map/ppermute | solution.py:494
  19.0 7.5 %collective-permute-start.4 = (f32[2,1080]{1,0:T(2,128)S(1)}, f32[2,1080]{1,0:T(2,128)S(1)}, u32[]{:S(2)}, u32[]{:S(2)}) collective-permute-start(f32[2,1080]{1,0:T(2,128)S(1)} %get-tuple-element.28), channel_id=1, source_target_pairs={{0,64},{64,0},{128,192},{192,128},{1,65},{65,1},{129,193},{193,129... | collective-permute-start | bytes 25928 | tf_op jit(solution)/shard_map/ppermute | solution.py:491
  19.0 7.5 %collective-permute-start.5 = (f32[2,1080]{1,0:T(2,128)S(1)}, f32[2,1080]{1,0:T(2,128)S(1)}, u32[]{:S(2)}, u32[]{:S(2)}) collective-permute-start(f32[2,1080]{1,0:T(2,128)S(1)} %get-tuple-element.29), channel_id=1, source_target_pairs={{64,128},{128,64},{0,32},{192,224},{65,129},{129,65},{1,33},{193,2... | collective-permute-start | bytes 25928 | tf_op jit(solution)/shard_map/ppermute | solution.py:492
  19.1 12.3 %collective-permute-start.6 = (f32[4,8,384]{2,1,0:T(8,128)S(1)}, f32[4,8,384]{2,1,0:T(8,128)S(1)}, u32[]{:S(2)}, u32[]{:S(2)}) collective-permute-start(f32[4,8,384]{2,1,0:T(8,128)S(1)} %get-tuple-element.32), channel_id=1, source_target_pairs={{0,1},{1,2},{2,3},{3,4},{4,5},{5,6},{6,7},{7,8},{8,9},{9,10},{10,1... | collective-permute-start | bytes 147464 | tf_op jit(solution)/shard_map/ppermute | solution.py:493
  20.6 10.8 %collective-permute-start.7 = (f32[4,8,384]{2,1,0:T(8,128)S(1)}, f32[4,8,384]{2,1,0:T(8,128)S(1)}, u32[]{:S(2)}, u32[]{:S(2)}) collective-permute-start(f32[4,8,384]{2,1,0:T(8,128)S(1)} %get-tuple-element.33), channel_id=1, source_target_pairs={{1,0},{2,1},{3,2},{4,3},{5,4},{6,5},{7,6},{8,7},{9,8},{10,9},{11,1... | collective-permute-start | bytes 147464 | tf_op jit(solution)/shard_map/ppermute | solution.py:494
  31.4 32.3 %copy-start.2 = (bf16[17,192,192]{2,1,0:T(8,128)(2,1)S(1)}, bf16[17,192,192]{2,1,0:T(8,128)(2,1)}, u32[]{:S(2)}) copy-start(bf16[17,192,192]{2,1,0:T(8,128)(2,1)} %constant.48.clone.mi_ref) | copy-start | bytes 3760132
  31.4 32.3 %copy-start.3 = (bf16[34,192,96]{2,1,0:T(8,128)(2,1)S(1)}, bf16[34,192,96]{2,1,0:T(8,128)(2,1)}, u32[]{:S(2)}) copy-start(bf16[34,192,96]{2,1,0:T(8,128)(2,1)} %constant.47.clone.mf_ref) | copy-start | bytes 3760132
  31.4 32.3 %copy-start.4 = (f32[17,96,128]{2,1,0:T(8,128)S(1)}, f32[17,96,128]{2,1,0:T(8,128)}, u32[]{:S(2)}) copy-start(f32[17,96,128]{2,1,0:T(8,128)} %constant.49.clone.sig_ref) | copy-start | bytes 2506756
  31.4 32.3 %copy-start.5 = (bf16[128,144]{1,0:T(8,128)(2,1)S(1)}, bf16[128,144]{1,0:T(8,128)(2,1)}, u32[]{:S(2)}) copy-start(bf16[128,144]{1,0:T(8,128)(2,1)} %constant.46.clone.inv_ref) | copy-start | bytes 110596
  31.5 32.2 %copy-start.7 = (bf16[80,192]{1,0:T(8,128)(2,1)S(1)}, bf16[80,192]{1,0:T(8,128)(2,1)}, u32[]{:S(2)}) copy-start(bf16[80,192]{1,0:T(8,128)(2,1)} %constant.45.clone.fwd_ref) | copy-start | bytes 92164
  31.5 32.2 %copy-start.9 = (s32[128]{0:T(128)S(1)}, s32[128]{0:T(128)}, u32[]{:S(2)}) copy-start(s32[128]{0:T(128)} %cut_ref.1) | copy-start | bytes 1540

commit v4 on v3

--- a/solution.py
+++ b/solution.py
@@ -160,7 +160,7 @@
         ext_ref[f, east] = from_east_ref[slot]
 
 
-CHUNKS = tuple((i, min(i + 5, SEG)) for i in range(0, SEG, 5))
+CHUNKS = tuple((i, min(i + 2, SEG)) for i in range(0, SEG, 2))
 
 
 def first_kernel(
@@ -214,8 +214,8 @@
     _, even, polar = lat_of(ids_ref)
     placed_ref[...] = placed_rows(got_first_ref, got_second_ref, edge_ref, even, polar)
     a, f, c, qc = (tab_ref[n : n + 1, :] for n in range(4))
-    for i in range(0, SEG, 6):
-        end = min(i + 6, SEG)
+    for i in range(0, SEG, 2):
+        end = min(i + 2, SEG)
         at = slice(i, end)
         u = r_ref[0, at] + placed_ref[0, at]
         v = r_ref[1, at] + placed_ref[1, at]

time: 106 us -> 106 us (level)
  no operation moved by 1% of the time
where the time goes in v4:
time: 106 us; the launch traced here: 105 us
  blocking collectives  60.4 us (57%)
  Pallas kernels  20.9 us (20%)
  starting transfers between devices  19.1 us (18%)
  local copies, waits for them, and re-layouts  1.86 us (2%)
  waiting for transfers between devices  1.82 us (2%)
    all_to_all x1, blocking collectives, per_device(): lax.all_to_all(message.reshape(64, MROWS, 128), 'lon', split_axis=0, conc...  32 us
    all_to_all x1, blocking collectives, per_device(): lax.all_to_all(answer, 'lon', split_axis=0, concat_axis=0, tiled=True)  28.4 us
    pallas_call x6, Pallas kernels, call(): pl.pallas_call(body, name=name, out_shape=outs, in_specs=list(specs), out...  20.9 us
    ppermute x2, starting transfers between devices, exchange(): lax.ppermute(west, 'lon', [((i + 1) % 64, i) for i in range(64)])  12.1 us
    ppermute x2, starting transfers between devices, exchange(): lax.ppermute(east, 'lon', [(i, (i + 1) % 64) for i in range(64)])  4.47 us
    ppermute x2, starting transfers between devices, exchange(): got_second = lax.ppermute(second, ('lat', 'lon'), pairs_second)  2.47 us
  transfers between devices with their start and end apart: 8, of which 1 were waited for; matrix products, arithmetic and copies ran while one was open for 0% of the time, Pallas kernels for 5%

profile of v4, /device:TPU:8, one launch (start us, length us, event | category | flops | bytes accessed | tf_op | source)
XLA Modules:
  0.0 104.7 jit_solution(17419693958351709204)
XLA Ops:
  0.0 0.1 pad_add_fusion.ids_ref
  0.1 1.8 %copy-done = f32[5,8,45,360]{3,1,2,0:T(8,128)S(1)} copy-done((f32[5,8,45,360]{3,1,2,0:T(8,128)S(1)}, f32[5,8,45,360]{3,1,2,0:T(8,128)}, u32[]{:S(2)}) %copy-start) | copy-done | bytes 2592024
  1.9 1.2 %edges.1 = (f32[4,8,384]{2,1,0:T(8,128)S(1)}, f32[4,8,384]{2,1,0:T(8,128)S(1)}, f32[2,1080]{1,0:T(2,128)S(1)}, f32[2,1080]{1,0:T(2,128)S(1)}) custom-call(s32[2]{0:T(128)S(1)} %pad_add_fusion.ids_ref, f32[5,45,8,360]{3,2,1,0:T(8,128)S(1)} %bitcast.6), custom_call_target="tpu_custom_call" | custom-call | flops 10000000 | bytes 8388608 | tf_op jit(solution)/shard_map/edges/pallas_call | solution.py:462
  3.1 0.1 collective-permute-start.2
  3.1 2.4 %collective-permute-start.3 = (f32[2,1080]{1,0:T(2,128)S(1)}, f32[2,1080]{1,0:T(2,128)S(1)}, u32[]{:S(2)}, u32[]{:S(2)}) collective-permute-start(f32[2,1080]{1,0:T(2,128)S(1)} %get-tuple-element.25), channel_id=1, source_target_pairs={{64,128},{128,64},{0,32},{192,224},{65,129},{129,65},{1,33},{193,2... | collective-permute-start | bytes 25928 | tf_op jit(solution)/shard_map/ppermute | solution.py:492
  5.5 3.0 %collective-permute-start = (f32[4,8,384]{2,1,0:T(8,128)S(1)}, f32[4,8,384]{2,1,0:T(8,128)S(1)}, u32[]{:S(2)}, u32[]{:S(2)}) collective-permute-start(f32[4,8,384]{2,1,0:T(8,128)S(1)} %get-tuple-element.22), channel_id=1, source_target_pairs={{0,1},{1,2},{2,3},{3,4},{4,5},{5,6},{6,7},{7,8},{8,9},{9,10},{10,1... | collective-permute-start | bytes 147464 | tf_op jit(solution)/shard_map/ppermute | solution.py:493
  8.5 6.1 %collective-permute-start.1 = (f32[4,8,384]{2,1,0:T(8,128)S(1)}, f32[4,8,384]{2,1,0:T(8,128)S(1)}, u32[]{:S(2)}, u32[]{:S(2)}) collective-permute-start(f32[4,8,384]{2,1,0:T(8,128)S(1)} %get-tuple-element.23), channel_id=1, source_target_pairs={{1,0},{2,1},{3,2},{4,3},{5,4},{6,5},{7,6},{8,7},{9,8},{10,9},{11,1... | collective-permute-start | bytes 147464 | tf_op jit(solution)/shard_map/ppermute | solution.py:494
  14.6 0.1 sine_abs_fusion.cos_ref
  14.7 0.1 cosine_multiply_fusion
  14.8 0.1 broadcast_divide_fusion
  14.9 0.0 collective-permute-done.2.got_first_ref
  14.9 0.0 collective-permute-done.3.got_second_ref
  14.9 1.8 %collective-permute-done.from_west_ref = f32[4,8,384]{2,1,0:T(8,128)S(1)} collective-permute-done((f32[4,8,384]{2,1,0:T(8,128)S(1)}, f32[4,8,384]{2,1,0:T(8,128)S(1)}, u32[]{:S(2)}, u32[]{:S(2)}) %collective-permute-start) | collective-permute-done | bytes 49184 | tf_op jit(solution)/shard_map/ppermute | solution.py:493
  16.7 0.0 collective-permute-done.1.from_east_ref
  16.7 2.3 %first.1 = (f32[5,45,8,384]{3,2,1,0:T(8,128)S(1)}, f32[4,8,384]{2,1,0:T(8,128)S(1)}, f32[4,8,384]{2,1,0:T(8,128)S(1)}, f32[2,1080]{1,0:T(2,128)S(1)}, f32[2,1080]{1,0:T(2,128)S(1)}) custom-call(s32[2]{0:T(128)S(1)} %pad_add_fusion.ids_ref, f32[5,45,8,360]{3,2,1,0:T(8,128)S(1)} %bitcast.7, f32[4,8,384]{2,1,0:T(8,128)S(1)} %collective-permute-done.from_west_ref, ...), custom_call_target="tpu_custom_call" | custom-call | flops 100000000 | bytes 8388608 | tf_op jit(solution)/shard_map/first/pallas_call | solution.py:462
  19.0 0.0 collective-permute-start.4
  19.0 0.1 collective-permute-start.5
  19.1 1.4 %collective-permute-start.6 = (f32[4,8,384]{2,1,0:T(8,128)S(1)}, f32[4,8,384]{2,1,0:T(8,128)S(1)}, u32[]{:S(2)}, u32[]{:S(2)}) collective-permute-start(f32[4,8,384]{2,1,0:T(8,128)S(1)} %get-tuple-element.32), channel_id=1, source_target_pairs={{0,1},{1,2},{2,3},{3,4},{4,5},{5,6},{6,7},{7,8},{8,9},{9,10},{10,1... | collective-permute-start | bytes 147464 | tf_op jit(solution)/shard_map/ppermute | solution.py:493
  20.6 6.0 %collective-permute-start.7 = (f32[4,8,384]{2,1,0:T(8,128)S(1)}, f32[4,8,384]{2,1,0:T(8,128)S(1)}, u32[]{:S(2)}, u32[]{:S(2)}) collective-permute-start(f32[4,8,384]{2,1,0:T(8,128)S(1)} %get-tuple-element.33), channel_id=1, source_target_pairs={{1,0},{2,1},{3,2},{4,3},{5,4},{6,5},{7,6},{8,7},{9,8},{10,9},{11,1... | collective-permute-start | bytes 147464 | tf_op jit(solution)/shard_map/ppermute | solution.py:494
  26.5 0.0 collective-permute-done.5.got_second_ref
  26.6 4.8 %pack.1 = (f32[8,8,23,128]{3,2,1,0:T(8,128)S(1)}, f32[4,45,8,384]{3,2,1,0:T(8,128)S(1)}, bf16[2688,512]{1,0:T(8,128)(2,1)S(1)}) custom-call(s32[2]{0:T(128)S(1)} %pad_add_fusion.ids_ref, s32[128]{0:T(128)S(1)} %copy-done.8, f32[5,45,8,384]{3,2,1,0:T(8,128)S(1)} %get-tuple-element.27.r_ref, f32[2,1080]{1,0:T(2,128)S(1)} %collective-permute-done.4.got_first_ref, ...), custom_call_target="tpu_custom_call" | custom-call | flops 1000000000 | bytes 8388608 | tf_op jit(solution)/shard_map/pack/pallas_call | solution.py:462
  31.4 0.0 copy-start.2
  31.4 0.0 copy-start.3
  31.4 0.0 copy-start.4
  31.5 0.0 copy-start.5
  31.5 0.0 copy-start.7
  31.5 0.0 copy-start.9
  31.5 0.2 zonal.1.zonal_ref
  31.7 32.0 %all_to_all.10.in_ref = f32[64,23,128]{2,1,0:T(8,128)S(1)} all-to-all(f32[64,23,128]{2,1,0:T(8,128)S(1)} %bitcast.9), channel_id=1, replica_groups=mesh['lat'=4,'lon'=64] {'lon'}, dimensions={0} | all-to-all | bytes 1507328 | tf_op jit(solution)/shard_map/all_to_all | solution.py:558
  63.7 7.5 %spectral.1 = f32[64,23,128]{2,1,0:T(8,128)S(1)} custom-call(s32[2]{0:T(128)S(1)} %pad_add_fusion.ids_ref, s32[128]{0:T(128)S(1)} %copy-done.8, s32[128]{0:T(128)S(1)} %copy-done.9, f32[1448]{0:T(1024)S(1)} %sine_abs_fusion.cos_ref, f32[64,23,128]{2,1,0:T(8,128)S(1)} %all_to_all.10.in_ref, s32[8,512]{1,0:T(8,128)S(1)} %copy-done.6, ...), custom_call_target="tpu_custom_call" | custom-call | flops 1000000000 | bytes 8388608 | tf_op jit(solution)/shard_map/spectral/pallas_call | solution.py:462
  71.3 28.4 %all_to_all.11 = f32[64,23,128]{2,1,0:T(8,128)S(1)} all-to-all(f32[64,23,128]{2,1,0:T(8,128)S(1)} %spectral.1), channel_id=1, replica_groups=mesh['lat'=4,'lon'=64] {'lon'}, dimensions={0} | all-to-all | bytes 1507328 | tf_op jit(solution)/shard_map/all_to_all | solution.py:571
  99.7 4.9 %final.1 = f32[5,45,8,360]{3,2,1,0:T(8,128)} custom-call(s32[2]{0:T(128)S(1)} %pad_add_fusion.ids_ref, s32[128]{0:T(128)S(1)} %copy-done.8, f32[8,8,23,128]{3,2,1,0:T(8,128)S(1)} %bitcast.8, f32[4,45,8,384]{3,2,1,0:T(8,128)S(1)} %get-tuple-element.31.p2_ref.next_ref, f32[2,45,8,384]{3,2,1,0:T(8,128)S(1)} %zonal.1.zonal_ref, f32[8,384]{1,0:T(8,128)S(1)} %stack.23.tab_ref, ...), custom_call_target="tpu_custom_call" | custom-call | flops 1000000000 | bytes 8388608 | tf_op jit(solution)/shard_map/final/pallas_call | solution.py:462
  (18 shorter events, 0.1 us)
Async XLA Ops:
  0.1 1.8 %copy-start = (f32[5,8,45,360]{3,1,2,0:T(8,128)S(1)}, f32[5,8,45,360]{3,1,2,0:T(8,128)}, u32[]{:S(2)}) copy-start(f32[5,8,45,360]{3,1,2,0:T(8,128)} %param.9) | copy-start | bytes 7776004
  1.9 14.8 %copy-start.1 = (f32[5,8,45,360]{3,1,2,0:T(8,128)S(1)}, f32[5,8,45,360]{3,1,2,0:T(8,128)}, u32[]{:S(2)}) copy-start(f32[5,8,45,360]{3,1,2,0:T(8,128)} %param.9) | copy-start | bytes 7776004
  1.9 24.7 %copy-start.6 = (s32[8,512]{1,0:T(8,128)S(1)}, s32[8,512]{1,0:T(8,128)}, u32[]{:S(2)}) copy-start(s32[8,512]{1,0:T(8,128)} %constant.44.clone.slot_ref) | copy-start | bytes 49156
  1.9 24.7 %copy-start.8 = (s32[128]{0:T(128)S(1)}, s32[128]{0:T(128)}, u32[]{:S(2)}) copy-start(s32[128]{0:T(128)} %rows_ref.5) | copy-start | bytes 1540
  3.1 11.8 %collective-permute-start.2 = (f32[2,1080]{1,0:T(2,128)S(1)}, f32[2,1080]{1,0:T(2,128)S(1)}, u32[]{:S(2)}, u32[]{:S(2)}) collective-permute-start(f32[2,1080]{1,0:T(2,128)S(1)} %get-tuple-element.24), channel_id=1, source_target_pairs={{0,64},{64,0},{128,192},{192,128},{1,65},{65,1},{129,193},{193,129... | collective-permute-start | bytes 25928 | tf_op jit(solution)/shard_map/ppermute | solution.py:491
  3.1 11.7 %collective-permute-start.3 = (f32[2,1080]{1,0:T(2,128)S(1)}, f32[2,1080]{1,0:T(2,128)S(1)}, u32[]{:S(2)}, u32[]{:S(2)}) collective-permute-start(f32[2,1080]{1,0:T(2,128)S(1)} %get-tuple-element.25), channel_id=1, source_target_pairs={{64,128},{128,64},{0,32},{192,224},{65,129},{129,65},{1,33},{193,2... | collective-permute-start | bytes 25928 | tf_op jit(solution)/shard_map/ppermute | solution.py:492
  5.5 11.2 %collective-permute-start = (f32[4,8,384]{2,1,0:T(8,128)S(1)}, f32[4,8,384]{2,1,0:T(8,128)S(1)}, u32[]{:S(2)}, u32[]{:S(2)}) collective-permute-start(f32[4,8,384]{2,1,0:T(8,128)S(1)} %get-tuple-element.22), channel_id=1, source_target_pairs={{0,1},{1,2},{2,3},{3,4},{4,5},{5,6},{6,7},{7,8},{8,9},{9,10},{10,1... | collective-permute-start | bytes 147464 | tf_op jit(solution)/shard_map/ppermute | solution.py:493
  8.5 8.1 %collective-permute-start.1 = (f32[4,8,384]{2,1,0:T(8,128)S(1)}, f32[4,8,384]{2,1,0:T(8,128)S(1)}, u32[]{:S(2)}, u32[]{:S(2)}) collective-permute-start(f32[4,8,384]{2,1,0:T(8,128)S(1)} %get-tuple-element.23), channel_id=1, source_target_pairs={{1,0},{2,1},{3,2},{4,3},{5,4},{6,5},{7,6},{8,7},{9,8},{10,9},{11,1... | collective-permute-start | bytes 147464 | tf_op jit(solution)/shard_map/ppermute | solution.py:494
  19.0 7.5 %collective-permute-start.4 = (f32[2,1080]{1,0:T(2,128)S(1)}, f32[2,1080]{1,0:T(2,128)S(1)}, u32[]{:S(2)}, u32[]{:S(2)}) collective-permute-start(f32[2,1080]{1,0:T(2,128)S(1)} %get-tuple-element.28), channel_id=1, source_target_pairs={{0,64},{64,0},{128,192},{192,128},{1,65},{65,1},{129,193},{193,129... | collective-permute-start | bytes 25928 | tf_op jit(solution)/shard_map/ppermute | solution.py:491
  19.0 7.5 %collective-permute-start.5 = (f32[2,1080]{1,0:T(2,128)S(1)}, f32[2,1080]{1,0:T(2,128)S(1)}, u32[]{:S(2)}, u32[]{:S(2)}) collective-permute-start(f32[2,1080]{1,0:T(2,128)S(1)} %get-tuple-element.29), channel_id=1, source_target_pairs={{64,128},{128,64},{0,32},{192,224},{65,129},{129,65},{1,33},{193,2... | collective-permute-start | bytes 25928 | tf_op jit(solution)/shard_map/ppermute | solution.py:492
  19.1 12.3 %collective-permute-start.6 = (f32[4,8,384]{2,1,0:T(8,128)S(1)}, f32[4,8,384]{2,1,0:T(8,128)S(1)}, u32[]{:S(2)}, u32[]{:S(2)}) collective-permute-start(f32[4,8,384]{2,1,0:T(8,128)S(1)} %get-tuple-element.32), channel_id=1, source_target_pairs={{0,1},{1,2},{2,3},{3,4},{4,5},{5,6},{6,7},{7,8},{8,9},{9,10},{10,1... | collective-permute-start | bytes 147464 | tf_op jit(solution)/shard_map/ppermute | solution.py:493
  20.6 10.8 %collective-permute-start.7 = (f32[4,8,384]{2,1,0:T(8,128)S(1)}, f32[4,8,384]{2,1,0:T(8,128)S(1)}, u32[]{:S(2)}, u32[]{:S(2)}) collective-permute-start(f32[4,8,384]{2,1,0:T(8,128)S(1)} %get-tuple-element.33), channel_id=1, source_target_pairs={{1,0},{2,1},{3,2},{4,3},{5,4},{6,5},{7,6},{8,7},{9,8},{10,9},{11,1... | collective-permute-start | bytes 147464 | tf_op jit(solution)/shard_map/ppermute | solution.py:494
  31.4 32.3 %copy-start.2 = (bf16[17,192,192]{2,1,0:T(8,128)(2,1)S(1)}, bf16[17,192,192]{2,1,0:T(8,128)(2,1)}, u32[]{:S(2)}) copy-start(bf16[17,192,192]{2,1,0:T(8,128)(2,1)} %constant.48.clone.mi_ref) | copy-start | bytes 3760132
  31.4 32.3 %copy-start.3 = (bf16[34,192,96]{2,1,0:T(8,128)(2,1)S(1)}, bf16[34,192,96]{2,1,0:T(8,128)(2,1)}, u32[]{:S(2)}) copy-start(bf16[34,192,96]{2,1,0:T(8,128)(2,1)} %constant.47.clone.mf_ref) | copy-start | bytes 3760132
  31.4 32.3 %copy-start.4 = (f32[17,96,128]{2,1,0:T(8,128)S(1)}, f32[17,96,128]{2,1,0:T(8,128)}, u32[]{:S(2)}) copy-start(f32[17,96,128]{2,1,0:T(8,128)} %constant.49.clone.sig_ref) | copy-start | bytes 2506756
  31.5 32.3 %copy-start.5 = (bf16[128,144]{1,0:T(8,128)(2,1)S(1)}, bf16[128,144]{1,0:T(8,128)(2,1)}, u32[]{:S(2)}) copy-start(bf16[128,144]{1,0:T(8,128)(2,1)} %constant.46.clone.inv_ref) | copy-start | bytes 110596
  31.5 32.2 %copy-start.7 = (bf16[80,192]{1,0:T(8,128)(2,1)S(1)}, bf16[80,192]{1,0:T(8,128)(2,1)}, u32[]{:S(2)}) copy-start(bf16[80,192]{1,0:T(8,128)(2,1)} %constant.45.clone.fwd_ref) | copy-start | bytes 92164
  31.5 32.2 %copy-start.9 = (s32[128]{0:T(128)S(1)}, s32[128]{0:T(128)}, u32[]{:S(2)}) copy-start(s32[128]{0:T(128)} %cut_ref.1) | copy-start | bytes 1540
